TPU v7x, 512 devices: a whole 4x4x16 slice. The times are simulated.
512 devices in a mesh: ctx: 64 (over z, x), head: 8 (over y, core).
Axes of the slice: x: 4, y: 4, z: 16, core: 2. Of those that a mesh axis runs over, the one named last changes fastest.
Arguments:
- queries: bfloat16 [16384, 4096], P('ctx', 'head'), may hold values from -15 to 15
- key_rows: bfloat16 [16384, 4096], P('ctx', 'head'), may hold values from -4 to 4
- value_rows: bfloat16 [16384, 4096], P('ctx', 'head'), may hold values from -32 to 32
- cotangent: bfloat16 [16384, 4096], P('ctx', 'head'), may hold values from -6 to 6
- norm_gain: float32 [4096], P('head'), may hold values from 0.1 to 1.9
- pairing: int32 [64], replicated, may hold values from 0 to 63, as said below
Outputs:
- mixed: bfloat16 [16384, 4096], P('ctx', 'head')
- grad_query: bfloat16 [16384, 4096], P('ctx', 'head')
- grad_key: bfloat16 [16384, 4096], P('ctx', 'head')
- grad_value: bfloat16 [16384, 4096], P('ctx', 'head')
Inputs may be any that keep to these rules, and one draw needn't show every extreme that they name: pairing is a permutation of the 64 blocks, and pairing[b] differs from b.
All inputs are finite; a program needn't handle non-finite values.
Results may differ from a plain program's by a relative error of at most 0.012.
Values may be sent and summed in bfloat16 or wider, within the bound.
A program may use at most 64 MiB of HBM per device.

v0:
```python
import math

import jax
import jax.numpy as jnp
from jax import lax
from jax.sharding import PartitionSpec as P

H = 32
HD = 128
BLOCK = 256


EPSILON = 1e-05


def from_behind(value, axis, steps):
    count = lax.axis_size(axis)
    first, last = (max(0, -steps), min(count, count - steps))
    return lax.ppermute(value, axis, [(source, source + steps) for source in range(first, last)])


def spread_rows(blocks_in, devices):
    return blocks_in.reshape(
        blocks_in.shape[0], devices, blocks_in.shape[1] // devices, blocks_in.shape[2]
    )


def choose_pieces(pieces, wanted, devices):
    holders = pieces.shape[0]
    stacked = pieces.reshape(holders * devices, pieces.shape[2], pieces.shape[3])
    wanted_grid = jnp.transpose(wanted.reshape(devices, -1))
    position = wanted_grid % holders * devices + wanted_grid // holders
    return jnp.take(stacked, position, axis=0)


def join_rows(pieces):
    return pieces.reshape(pieces.shape[0], pieces.shape[1] * pieces.shape[2], pieces.shape[3])


def window_scores(query_blocks, keys_window, first_block):
    blocks_here = query_blocks.shape[0]
    length = query_blocks.shape[1]
    factor = 1.0 / math.sqrt(query_blocks.shape[3])
    scores = (
        jnp.einsum("bihd,bjhd->bhij", query_blocks, keys_window, preferred_element_type=jnp.float32)
        * factor
    )
    places = jnp.arange(length)
    causal = places[:, None] >= places[None, :]
    earlier = first_block + jnp.arange(blocks_here) > 0
    earlier_mask = jnp.broadcast_to(earlier[:, None, None], (blocks_here, length, length))
    causal_mask = causal[None]
    partner_mask = jnp.ones((blocks_here, length, length), bool)
    allowed = jnp.concatenate([earlier_mask, causal_mask, partner_mask], axis=2)
    return jnp.where(allowed[:, None], scores, -jnp.inf)


def on_device(queries, key_rows, value_rows, cotangent, norm_gain, pairing):
    devices = lax.axis_size("ctx")
    my_index = lax.axis_index("ctx")
    width = queries.shape[1]
    heads_here = width // HD
    blocks_here = queries.shape[0] // BLOCK
    all_blocks = pairing.shape[0]
    shape_four = (blocks_here, BLOCK, heads_here, HD)
    key_blocks = key_rows.reshape(blocks_here, BLOCK, width)
    value_blocks = value_rows.reshape(blocks_here, BLOCK, width)
    arrived = (
        lax.all_to_all(
            spread_rows(key_blocks, devices), "ctx", split_axis=1, concat_axis=1, tiled=True
        ),
        lax.all_to_all(
            spread_rows(value_blocks, devices), "ctx", split_axis=1, concat_axis=1, tiled=True
        ),
    )
    block_range = jnp.arange(all_blocks, dtype=jnp.int32)
    delivered = (
        lax.all_to_all(
            choose_pieces(arrived[0], pairing, devices),
            "ctx",
            split_axis=1,
            concat_axis=1,
            tiled=True,
        ),
        lax.all_to_all(
            choose_pieces(arrived[1], pairing, devices),
            "ctx",
            split_axis=1,
            concat_axis=1,
            tiled=True,
        ),
    )
    partner_keys = join_rows(delivered[0])
    partner_values = join_rows(delivered[1])
    trailing = from_behind((key_blocks[-1], value_blocks[-1]), "ctx", 1)
    prior_keys = jnp.concatenate([trailing[0][None], key_blocks[:-1]], axis=0)
    prior_values = jnp.concatenate([trailing[1][None], value_blocks[:-1]], axis=0)
    keys_window = jnp.concatenate([prior_keys, key_blocks, partner_keys], axis=1).reshape(
        blocks_here, 3 * BLOCK, heads_here, HD
    )
    values_window = jnp.concatenate([prior_values, value_blocks, partner_values], axis=1).reshape(
        blocks_here, 3 * BLOCK, heads_here, HD
    )
    query_blocks = queries.reshape(shape_four)
    first_block = my_index * blocks_here
    scores = window_scores(query_blocks, keys_window, first_block)
    highest = jnp.max(scores, axis=-1, keepdims=True)
    logsum = highest + jnp.log(jnp.sum(jnp.exp(scores - highest), axis=-1, keepdims=True))
    weights = jnp.exp(scores - logsum)
    weights_low = weights.astype(jnp.bfloat16)
    attn = jnp.einsum(
        "bhij,bjhd->bihd", weights_low, values_window, preferred_element_type=jnp.float32
    ).astype(jnp.bfloat16)
    attn_flat = attn.reshape(blocks_here * BLOCK, width).astype(jnp.float32)
    grad_in = norm_gain * cotangent.astype(jnp.float32)
    squares, products = lax.psum(
        (jnp.sum(attn_flat * attn_flat, axis=1), jnp.sum(grad_in * attn_flat, axis=1)), "head"
    )
    features = float(H * HD)
    rms_scale = lax.rsqrt(squares / features + EPSILON)[:, None]
    mixed = (attn_flat * rms_scale * norm_gain).astype(jnp.bfloat16)
    dattn = (
        rms_scale * grad_in - attn_flat * rms_scale**3 * (products / features)[:, None]
    ).astype(jnp.bfloat16)
    dattn_four = dattn.reshape(shape_four)
    delta = jnp.einsum("bihd,bihd->bih", dattn_four, attn, preferred_element_type=jnp.float32)
    dprob = jnp.einsum(
        "bihd,bjhd->bhij", dattn_four, values_window, preferred_element_type=jnp.float32
    )
    dscore = (weights * (dprob - jnp.transpose(delta, (0, 2, 1))[..., None])).astype(jnp.bfloat16)
    factor = 1.0 / math.sqrt(HD)
    grad_query = (
        jnp.einsum("bhij,bjhd->bihd", dscore, keys_window, preferred_element_type=jnp.float32)
        * factor
    ).astype(jnp.bfloat16)
    key_terms = (
        (
            jnp.einsum("bhij,bihd->bjhd", dscore, query_blocks, preferred_element_type=jnp.float32)
            * factor
        )
        .astype(jnp.bfloat16)
        .reshape(blocks_here, 3 * BLOCK, width)
    )
    value_terms = (
        jnp.einsum("bhij,bihd->bjhd", weights_low, dattn_four, preferred_element_type=jnp.float32)
        .astype(jnp.bfloat16)
        .reshape(blocks_here, 3 * BLOCK, width)
    )
    inverse = jnp.zeros((all_blocks,), jnp.int32).at[pairing].set(block_range)
    returned = (
        lax.all_to_all(
            spread_rows(key_terms[:, 2 * BLOCK :], devices),
            "ctx",
            split_axis=1,
            concat_axis=1,
            tiled=True,
        ),
        lax.all_to_all(
            spread_rows(value_terms[:, 2 * BLOCK :], devices),
            "ctx",
            split_axis=1,
            concat_axis=1,
            tiled=True,
        ),
    )
    homeward = (
        lax.all_to_all(
            choose_pieces(returned[0], inverse, devices),
            "ctx",
            split_axis=1,
            concat_axis=1,
            tiled=True,
        ),
        lax.all_to_all(
            choose_pieces(returned[1], inverse, devices),
            "ctx",
            split_axis=1,
            concat_axis=1,
            tiled=True,
        ),
    )
    partner_key_part = join_rows(homeward[0])
    partner_value_part = join_rows(homeward[1])
    leading = from_behind((key_terms[0, :BLOCK], value_terms[0, :BLOCK]), "ctx", -1)
    next_key_part = jnp.concatenate([key_terms[1:, :BLOCK], leading[0][None]], axis=0)
    next_value_part = jnp.concatenate([value_terms[1:, :BLOCK], leading[1][None]], axis=0)
    own_keys = key_terms[:, BLOCK : 2 * BLOCK].astype(jnp.float32)
    own_values = value_terms[:, BLOCK : 2 * BLOCK].astype(jnp.float32)
    grad_key = (
        own_keys + next_key_part.astype(jnp.float32) + partner_key_part.astype(jnp.float32)
    ).astype(jnp.bfloat16)
    grad_value = (
        own_values + next_value_part.astype(jnp.float32) + partner_value_part.astype(jnp.float32)
    ).astype(jnp.bfloat16)
    rows_here = blocks_here * BLOCK
    return (
        mixed,
        grad_query.reshape(rows_here, width),
        grad_key.reshape(rows_here, width),
        grad_value.reshape(rows_here, width),
    )


def solution(mesh):
    placed = (
        P("ctx", "head"),
        P("ctx", "head"),
        P("ctx", "head"),
        P("ctx", "head"),
        P("head"),
        P(),
    )
    return jax.shard_map(
        on_device,
        mesh=mesh,
        in_specs=placed,
        out_specs=(P("ctx", "head"), P("ctx", "head"), P("ctx", "head"), P("ctx", "head")),
        check_vma=False,
    )
```

profile of v0, /device:TPU:6, one launch (start us, length us, event | category | flops | bytes accessed | tf_op | source)
XLA Modules:
  0.0 270.7 jit_solution(4396580896431884058)
XLA Ops:
  0.7 1.8 reshape_reshape.7
  2.4 18.6 %all-to-all-start.2 = ((bf16[1,64,4,512]{3,2,0,1:T(4,128)(2,1)}), bf16[1,64,4,512]{3,2,0,1:T(4,128)(2,1)S(1)}, u32[]{:S(2)}, u32[]{:S(2)}) async-start(bf16[1,64,4,512]{3,2,0,1:T(4,128)(2,1)} %reshape_reshape.7), calls=%async_computation.2 | async-start | bytes 524288 | tf_op jit(solution)/shard_map/all_to_all | solution.py:69
  21.0 1.7 reshape_reshape.6
  22.8 19.8 %all-to-all-done.2 = bf16[1,64,4,512]{3,2,0,1:T(4,128)(2,1)S(1)} async-done(((bf16[1,64,4,512]{3,2,0,1:T(4,128)(2,1)}), bf16[1,64,4,512]{3,2,0,1:T(4,128)(2,1)S(1)}, u32[]{:S(2)}, u32[]{:S(2)}) %all-to-all-start.2) | async-done | bytes 262176 | tf_op jit(solution)/shard_map/all_to_all | solution.py:69
  42.5 5.9 %all-to-all-start = ((bf16[1,64,4,512]{3,2,0,1:T(4,128)(2,1)}), bf16[1,64,4,512]{3,2,0,1:T(4,128)(2,1)S(1)}, u32[]{:S(2)}, u32[]{:S(2)}) async-start(bf16[1,64,4,512]{3,2,0,1:T(4,128)(2,1)} %reshape_reshape.6), calls=%async_computation | async-start | bytes 524288 | tf_op jit(solution)/shard_map/all_to_all | solution.py:72
  48.5 0.7 fusion.16
  49.1 0.7 and_bitcast_fusion.1
  49.8 0.8 gather_fusion.1
  50.6 18.5 %all-to-all-done = bf16[1,64,4,512]{3,2,0,1:T(4,128)(2,1)S(1)} async-done(((bf16[1,64,4,512]{3,2,0,1:T(4,128)(2,1)}), bf16[1,64,4,512]{3,2,0,1:T(4,128)(2,1)S(1)}, u32[]{:S(2)}, u32[]{:S(2)}) %all-to-all-start) | async-done | bytes 262176 | tf_op jit(solution)/shard_map/all_to_all | solution.py:72
  69.1 0.8 gather_fusion
  69.9 1.1 fusion.12
  71.0 5.9 %all-to-all-start.3 = ((bf16[1,64,4,512]{3,2,0,1:T(4,128)(2,1)}), bf16[1,64,4,512]{3,2,0,1:T(4,128)(2,1)S(1)}, u32[]{:S(2)}, u32[]{:S(2)}) async-start(bf16[1,64,4,512]{3,2,0,1:T(4,128)(2,1)} %get-tuple-element.31), calls=%async_computation.3 | async-start | bytes 524288 | tf_op jit(solution)/shard_map/all_to_all | solution.py:78
  77.0 3.4 %collective-permute-start = (bf16[256,512]{1,0:T(8,128)(2,1)S(1)}, bf16[256,512]{1,0:T(8,128)(2,1)S(1)}, u32[]{:S(2)}, u32[]{:S(2)}) collective-permute-start(bf16[256,512]{1,0:T(8,128)(2,1)S(1)} %copy-done.5), channel_id=1, source_target_pairs={{0,8},{8,16},{16,24},{24,32},{32,40},{40,48},{48,56},{56,64},{64,7... | collective-permute-start | bytes 786440 | tf_op jit(solution)/shard_map/ppermute | solution.py:19
  80.5 3.4 %collective-permute-start.1 = (bf16[256,512]{0,1:T(8,128)(2,1)S(1)}, bf16[256,512]{0,1:T(8,128)(2,1)S(1)}, u32[]{:S(2)}, u32[]{:S(2)}) collective-permute-start(bf16[256,512]{0,1:T(8,128)(2,1)S(1)} %copy.64), channel_id=1, source_target_pairs={{0,8},{8,16},{16,24},{24,32},{32,40},{40,48},{48,56},{56,64},{64,7... | collective-permute-start | bytes 786440 | tf_op jit(solution)/shard_map/ppermute | solution.py:19
  83.9 0.8 copy.61
  84.9 0.8 copy.68
  85.8 12.6 %all-to-all-done.3 = bf16[1,64,4,512]{3,2,0,1:T(4,128)(2,1)S(1)} async-done(((bf16[1,64,4,512]{3,2,0,1:T(4,128)(2,1)}), bf16[1,64,4,512]{3,2,0,1:T(4,128)(2,1)S(1)}, u32[]{:S(2)}, u32[]{:S(2)}) %all-to-all-start.3) | async-done | bytes 262176 | tf_op jit(solution)/shard_map/all_to_all | solution.py:78
  98.4 6.1 %all-to-all-start.1 = ((bf16[1,64,4,512]{3,2,0,1:T(4,128)(2,1)}), bf16[1,64,4,512]{3,2,0,1:T(4,128)(2,1)}, u32[]{:S(2)}, u32[]{:S(2)}) async-start(bf16[1,64,4,512]{3,2,0,1:T(4,128)(2,1)} %get-tuple-element.32), calls=%async_computation.1 | async-start | bytes 524288 | tf_op jit(solution)/shard_map/all_to_all | solution.py:85
  104.5 0.9 add_bitcast_fusion
  105.5 0.8 copy.67
  106.3 0.9 copy.60
  107.3 0.7 copy-done.12
  108.0 1.7 fusion.1
  109.7 0.7 exponential_reduce_fusion
  110.4 13.2 %all-to-all-done.1 = bf16[1,64,4,512]{3,2,0,1:T(4,128)(2,1)} async-done(((bf16[1,64,4,512]{3,2,0,1:T(4,128)(2,1)}), bf16[1,64,4,512]{3,2,0,1:T(4,128)(2,1)}, u32[]{:S(2)}, u32[]{:S(2)}) %all-to-all-start.1) | async-done | bytes 262176 | tf_op jit(solution)/shard_map/all_to_all | solution.py:85
  123.6 1.8 concatenate.25
  125.4 1.8 copy.63
  127.2 3.0 %bitcast_convert_fusion = (f32[1,256,4,128]{1,3,2,0:T(8,128)}, bf16[4,128,256]{2,1,0:T(8,128)(2,1)}) fusion(f32[4,768,256]{2,1,0:T(8,128)S(1)} %get-tuple-element.34, f32[4,256]{1,0:T(4,128)S(1)} %log_add_fusion, pred[256,768]{0,1:T(8,128)(4,1)} %add_bitcast_fusion, bf16[1,256,4,128]{1,3,2,0:T(8,128)(2,1)} %copy.63, bf16[1,256,4,128]{1,3,2,0:T(8,128)(2,1)} %bitcast.155, ...), kind=kOutput, calls=%fused_computation.38 | convolution fusion | flops 207093760 | bytes 4919296 | tf_op jit(solution)/shard_map/bhij,bjhd->bihd/dot_general | solution.py:111
  130.2 1.3 copy.72
  131.5 1.0 multiply_reduce_fusion.2
  132.5 1.1 multiply_reduce_fusion.1
  133.6 12.4 %all-reduce = (f32[256]{0:T(256)S(1)}, f32[256]{0:T(256)S(1)}) all-reduce(f32[256]{0:T(256)S(1)} %multiply_reduce_fusion.1, f32[256]{0:T(256)S(1)} %multiply_reduce_fusion.2), channel_id=1, replica_groups=mesh['ctx'=64,'head'=8] {'head'}, use_global_device_ids=true, to_apply=%region_5.7 | all-reduce | flops 512 | bytes 4096 | tf_op jit(solution)/shard_map/psum | solution.py:116
  146.0 1.8 subtract_convert_fusion
  148.0 0.2 copy.87
  148.1 1.0 copy.101
  149.1 2.9 %convolution_convert_fusion = bf16[4,128,768]{2,1,0:T(8,128)(2,1)S(1)} fusion(bf16[256,4,128]{0,2,1:T(8,128)(2,1)S(1)} %copy.87, f32[4,768,256]{2,1,0:T(8,128)} %copy-done, f32[4,256]{1,0:T(4,128)S(1)} %log_add_fusion, pred[256,768]{0,1:T(8,128)(4,1)S(1)} %copy-done.9), kind=kOutput, calls=%fused_computation.12 | convolution fusion | flops 204865536 | bytes 4395008 | tf_op jit(solution)/shard_map/bhij,bihd->bjhd/dot_general | solution.py:145
  152.0 0.9 fusion.24
  152.9 2.1 copy.111
  155.0 1.7 reshape.284
  156.7 6.6 %all-to-all-start.6 = ((bf16[1,64,4,512]{3,2,0,1:T(4,128)(2,1)}), bf16[1,64,4,512]{3,2,0,1:T(4,128)(2,1)}, u32[]{:S(2)}, u32[]{:S(2)}) async-start(bf16[1,64,4,512]{3,2,0,1:T(4,128)(2,1)} %bitcast.152), calls=%async_computation.6 | async-start | bytes 524288 | tf_op jit(solution)/shard_map/all_to_all | solution.py:158
  163.3 1.2 multiply_reduce_fusion
  164.5 2.4 multiply_convert_fusion
  166.9 0.6 multiply_convert_fusion.1
  167.6 0.4 copy-done.2
  168.2 0.8 reshape.280
  169.0 16.3 %all-to-all-done.6 = bf16[1,64,4,512]{3,2,0,1:T(4,128)(2,1)} async-done(((bf16[1,64,4,512]{3,2,0,1:T(4,128)(2,1)}), bf16[1,64,4,512]{3,2,0,1:T(4,128)(2,1)}, u32[]{:S(2)}, u32[]{:S(2)}) %all-to-all-start.6) | async-done | bytes 262176 | tf_op jit(solution)/shard_map/all_to_all | solution.py:158
  185.3 6.0 %all-to-all-start.4 = ((bf16[1,64,4,512]{3,2,0,1:T(4,128)(2,1)}), bf16[1,64,4,512]{3,2,0,1:T(4,128)(2,1)S(1)}, u32[]{:S(2)}, u32[]{:S(2)}) async-start(bf16[1,64,4,512]{3,2,0,1:T(4,128)(2,1)} %bitcast.41), calls=%async_computation.4 | async-start | bytes 524288 | tf_op jit(solution)/shard_map/all_to_all | solution.py:151
  191.3 0.8 scatter_custom_fusion
  192.1 1.7 gather_fusion.3
  193.8 18.5 %all-to-all-done.4 = bf16[1,64,4,512]{3,2,0,1:T(4,128)(2,1)S(1)} async-done(((bf16[1,64,4,512]{3,2,0,1:T(4,128)(2,1)}), bf16[1,64,4,512]{3,2,0,1:T(4,128)(2,1)S(1)}, u32[]{:S(2)}, u32[]{:S(2)}) %all-to-all-start.4) | async-done | bytes 262176 | tf_op jit(solution)/shard_map/all_to_all | solution.py:151
  212.4 0.8 gather_fusion.2
  213.2 1.0 fusion.10
  214.2 26.4 %all_to_all.40 = bf16[1,64,4,512]{3,2,0,1:T(4,128)(2,1)S(1)} all-to-all(bf16[1,64,4,512]{3,2,0,1:T(4,128)(2,1)S(1)} %get-tuple-element.30), channel_id=1, replica_groups=mesh['ctx'=64,'head'=8] {'ctx'}, dimensions={1} | all-to-all | bytes 524288 | tf_op jit(solution)/shard_map/all_to_all | solution.py:167
  240.6 6.1 %all-to-all-start.7 = ((bf16[1,64,4,512]{3,2,0,1:T(4,128)(2,1)}), bf16[1,64,4,512]{3,2,0,1:T(4,128)(2,1)S(1)}, u32[]{:S(2)}, u32[]{:S(2)}) async-start(bf16[1,64,4,512]{3,2,0,1:T(4,128)(2,1)} %get-tuple-element.29), calls=%async_computation.7 | async-start | bytes 524288 | tf_op jit(solution)/shard_map/all_to_all | solution.py:174
  246.7 0.9 copy.107
  247.6 2.8 %collective-permute-start.2 = (bf16[256,512]{1,0:T(8,128)(2,1)}, bf16[256,512]{1,0:T(8,128)(2,1)S(1)}, u32[]{:S(2)}, u32[]{:S(2)}) collective-permute-start(bf16[256,512]{1,0:T(8,128)(2,1)} %bitcast.161), channel_id=1, source_target_pairs={{8,0},{16,8},{24,16},{32,24},{40,32},{48,40},{56,48},{64,56},{72,6... | collective-permute-start | bytes 786440 | tf_op jit(solution)/shard_map/ppermute | solution.py:19
  250.3 0.8 copy.110
  251.2 2.5 collective-permute-start.3
  253.7 2.2 fusion.2
  255.9 1.8 copy.94
  258.0 9.4 %all-to-all-done.7 = bf16[1,64,4,512]{3,2,0,1:T(4,128)(2,1)S(1)} async-done(((bf16[1,64,4,512]{3,2,0,1:T(4,128)(2,1)}), bf16[1,64,4,512]{3,2,0,1:T(4,128)(2,1)S(1)}, u32[]{:S(2)}, u32[]{:S(2)}) %all-to-all-start.7) | async-done | bytes 262176 | tf_op jit(solution)/shard_map/all_to_all | solution.py:174
  267.4 0.8 fusion.8
  268.2 1.6 collective-permute-done.3
  269.9 0.8 fusion.9
  (57 shorter events, 1.2 us)
Async XLA Ops:
  0.6 79.7 %copy-start.4 = (bf16[256,512]{1,0:T(8,128)(2,1)S(1)}, bf16[256,512]{1,0:T(8,128)(2,1)}, u32[]{:S(2)}) copy-start(bf16[256,512]{1,0:T(8,128)(2,1)} %param.9) | copy-start | bytes 786436
  0.6 76.3 %copy-start.5 = (bf16[256,512]{1,0:T(8,128)(2,1)S(1)}, bf16[256,512]{1,0:T(8,128)(2,1)}, u32[]{:S(2)}) copy-start(bf16[256,512]{1,0:T(8,128)(2,1)} %param.10) | copy-start | bytes 786436
  0.7 84.1 %copy-start.10 = (bf16[256,512]{1,0:T(8,128)(2,1)S(1)}, bf16[256,512]{1,0:T(8,128)(2,1)}, u32[]{:S(2)}) copy-start(bf16[256,512]{1,0:T(8,128)(2,1)} %param.8) | copy-start | bytes 786436
  2.4 40.1 %all-to-all-start.2 = ((bf16[1,64,4,512]{3,2,0,1:T(4,128)(2,1)}), bf16[1,64,4,512]{3,2,0,1:T(4,128)(2,1)S(1)}, u32[]{:S(2)}, u32[]{:S(2)}) async-start(bf16[1,64,4,512]{3,2,0,1:T(4,128)(2,1)} %reshape_reshape.7), calls=%async_computation.2 | async-start | bytes 524288 | tf_op jit(solution)/shard_map/all_to_all | solution.py:69
  42.5 26.6 %all-to-all-start = ((bf16[1,64,4,512]{3,2,0,1:T(4,128)(2,1)}), bf16[1,64,4,512]{3,2,0,1:T(4,128)(2,1)S(1)}, u32[]{:S(2)}, u32[]{:S(2)}) async-start(bf16[1,64,4,512]{3,2,0,1:T(4,128)(2,1)} %reshape_reshape.6), calls=%async_computation | async-start | bytes 524288 | tf_op jit(solution)/shard_map/all_to_all | solution.py:72
  71.0 27.4 %all-to-all-start.3 = ((bf16[1,64,4,512]{3,2,0,1:T(4,128)(2,1)}), bf16[1,64,4,512]{3,2,0,1:T(4,128)(2,1)S(1)}, u32[]{:S(2)}, u32[]{:S(2)}) async-start(bf16[1,64,4,512]{3,2,0,1:T(4,128)(2,1)} %get-tuple-element.31), calls=%async_computation.3 | async-start | bytes 524288 | tf_op jit(solution)/shard_map/all_to_all | solution.py:78
  77.0 29.3 %collective-permute-start = (bf16[256,512]{1,0:T(8,128)(2,1)S(1)}, bf16[256,512]{1,0:T(8,128)(2,1)S(1)}, u32[]{:S(2)}, u32[]{:S(2)}) collective-permute-start(bf16[256,512]{1,0:T(8,128)(2,1)S(1)} %copy-done.5), channel_id=1, source_target_pairs={{0,8},{8,16},{16,24},{24,32},{32,40},{40,48},{48,56},{56,64},{64,7... | collective-permute-start | bytes 786440 | tf_op jit(solution)/shard_map/ppermute | solution.py:19
  80.5 25.0 %collective-permute-start.1 = (bf16[256,512]{0,1:T(8,128)(2,1)S(1)}, bf16[256,512]{0,1:T(8,128)(2,1)S(1)}, u32[]{:S(2)}, u32[]{:S(2)}) collective-permute-start(bf16[256,512]{0,1:T(8,128)(2,1)S(1)} %copy.64), channel_id=1, source_target_pairs={{0,8},{8,16},{16,24},{24,32},{32,40},{40,48},{48,56},{56,64},{64,7... | collective-permute-start | bytes 786440 | tf_op jit(solution)/shard_map/ppermute | solution.py:19
  98.4 25.2 %all-to-all-start.1 = ((bf16[1,64,4,512]{3,2,0,1:T(4,128)(2,1)}), bf16[1,64,4,512]{3,2,0,1:T(4,128)(2,1)}, u32[]{:S(2)}, u32[]{:S(2)}) async-start(bf16[1,64,4,512]{3,2,0,1:T(4,128)(2,1)} %get-tuple-element.32), calls=%async_computation.1 | async-start | bytes 524288 | tf_op jit(solution)/shard_map/all_to_all | solution.py:85
  107.3 2.5 copy-start.8
  107.3 0.7 copy-start.12
  109.7 20.5 %copy-start = (f32[4,768,256]{2,1,0:T(8,128)}, f32[4,768,256]{2,1,0:T(8,128)S(1)}, u32[]{:S(2)}) copy-start(f32[4,768,256]{2,1,0:T(8,128)S(1)} %get-tuple-element.34) | copy-start | bytes 9437188
  127.2 5.3 %copy-start.14 = (f32[512]{0:T(512)S(1)}, f32[512]{0:T(512)}, u32[]{:S(2)}) copy-start(f32[512]{0:T(512)} %param.12) | copy-start | bytes 6148
  130.2 18.9 %copy-start.9 = (pred[256,768]{0,1:T(8,128)(4,1)S(1)}, pred[256,768]{0,1:T(8,128)(4,1)}, u32[]{:S(2)}) copy-start(pred[256,768]{0,1:T(8,128)(4,1)} %add_bitcast_fusion) | copy-start | bytes 589828
  148.1 1.0 copy-start.13
  152.0 12.5 %copy-start.1 = (f32[4,768,256]{2,1,0:T(8,128)S(1)}, f32[4,768,256]{2,1,0:T(8,128)}, u32[]{:S(2)}) copy-start(f32[4,768,256]{2,1,0:T(8,128)} %copy-done) | copy-start | bytes 9437188
  156.7 28.5 %all-to-all-start.6 = ((bf16[1,64,4,512]{3,2,0,1:T(4,128)(2,1)}), bf16[1,64,4,512]{3,2,0,1:T(4,128)(2,1)}, u32[]{:S(2)}, u32[]{:S(2)}) async-start(bf16[1,64,4,512]{3,2,0,1:T(4,128)(2,1)} %bitcast.152), calls=%async_computation.6 | async-start | bytes 524288 | tf_op jit(solution)/shard_map/all_to_all | solution.py:158
  166.9 1.2 copy-start.2
  166.9 24.3 %copy-start.15 = (s32[64]{0:T(128)S(1)}, s32[64]{0:T(128)}, u32[]{:S(2)}) copy-start(s32[64]{0:T(128)} %param.13) | copy-start | bytes 772
  167.6 82.8 %copy-start.7 = (bf16[1,256,512]{1,2,0:T(8,128)(2,1)S(1)}, bf16[1,256,512]{1,2,0:T(8,128)(2,1)}, u32[]{:S(2)}) copy-start(bf16[1,256,512]{1,2,0:T(8,128)(2,1)} %get-tuple-element.19) | copy-start | bytes 786436
  168.0 85.6 %copy-start.11 = (bf16[1,256,4,128]{3,1,2,0:T(8,128)(2,1)S(1)}, bf16[1,256,4,128]{3,1,2,0:T(8,128)(2,1)}, u32[]{:S(2)}) copy-start(bf16[1,256,4,128]{3,1,2,0:T(8,128)(2,1)} %copy.68) | copy-start | bytes 786436
  168.1 85.6 %copy-start.3 = (bf16[4,256,768]{1,2,0:T(8,128)(2,1)S(1)}, bf16[4,256,768]{1,2,0:T(8,128)(2,1)}, u32[]{:S(2)}) copy-start(bf16[4,256,768]{1,2,0:T(8,128)(2,1)} %copy-done.2) | copy-start | bytes 4718596
  185.3 27.1 %all-to-all-start.4 = ((bf16[1,64,4,512]{3,2,0,1:T(4,128)(2,1)}), bf16[1,64,4,512]{3,2,0,1:T(4,128)(2,1)S(1)}, u32[]{:S(2)}, u32[]{:S(2)}) async-start(bf16[1,64,4,512]{3,2,0,1:T(4,128)(2,1)} %bitcast.41), calls=%async_computation.4 | async-start | bytes 524288 | tf_op jit(solution)/shard_map/all_to_all | solution.py:151
  240.6 17.2 %copy-start.6 = (bf16[1,256,512]{1,2,0:T(8,128)(2,1)S(1)}, bf16[1,256,512]{1,2,0:T(8,128)(2,1)}, u32[]{:S(2)}) copy-start(bf16[1,256,512]{1,2,0:T(8,128)(2,1)} %get-tuple-element.20) | copy-start | bytes 786436
  240.6 26.7 %all-to-all-start.7 = ((bf16[1,64,4,512]{3,2,0,1:T(4,128)(2,1)}), bf16[1,64,4,512]{3,2,0,1:T(4,128)(2,1)S(1)}, u32[]{:S(2)}, u32[]{:S(2)}) async-start(bf16[1,64,4,512]{3,2,0,1:T(4,128)(2,1)} %get-tuple-element.29), calls=%async_computation.7 | async-start | bytes 524288 | tf_op jit(solution)/shard_map/all_to_all | solution.py:174
  247.6 19.8 %collective-permute-start.2 = (bf16[256,512]{1,0:T(8,128)(2,1)}, bf16[256,512]{1,0:T(8,128)(2,1)S(1)}, u32[]{:S(2)}, u32[]{:S(2)}) collective-permute-start(bf16[256,512]{1,0:T(8,128)(2,1)} %bitcast.161), channel_id=1, source_target_pairs={{8,0},{16,8},{24,16},{32,24},{40,32},{48,40},{56,48},{64,56},{72,6... | collective-permute-start | bytes 786440 | tf_op jit(solution)/shard_map/ppermute | solution.py:19
  251.2 18.7 %collective-permute-start.3 = (bf16[256,512]{1,0:T(8,128)(2,1)}, bf16[256,512]{1,0:T(8,128)(2,1)S(1)}, u32[]{:S(2)}, u32[]{:S(2)}) collective-permute-start(bf16[256,512]{1,0:T(8,128)(2,1)} %bitcast.160), channel_id=1, source_target_pairs={{8,0},{16,8},{24,16},{32,24},{40,32},{48,40},{56,48},{64,56},{72,6... | collective-permute-start | bytes 786440 | tf_op jit(solution)/shard_map/ppermute | solution.py:19
where the time goes:
time: 272 us; the launch traced here: 271 us
  waiting for transfers between devices  110 us (40%)
  starting transfers between devices  67 us (25%)
  blocking collectives  38.8 us (14%)
  local copies, waits for them, and re-layouts  28.9 us (11%)
  matrix products  12.8 us (5%)
  other arithmetic  12 us (4%)
    all_to_all x1, blocking collectives, on_device(): lax.all_to_all(choose_pieces(returned[0], inverse, devices), 'ctx', split...  26.4 us
    all_to_all x1, waiting for transfers between devices, on_device(): lax.all_to_all(spread_rows(key_blocks, devices), 'ctx', split_axis=1, con...  19.8 us
    all_to_all x1, starting transfers between devices, on_device(): lax.all_to_all(spread_rows(key_blocks, devices), 'ctx', split_axis=1, con...  18.6 us
    all_to_all x1, waiting for transfers between devices, on_device(): lax.all_to_all(spread_rows(key_terms[:, 2 * BLOCK:], devices), 'ctx', spl...  18.5 us
    all_to_all x1, waiting for transfers between devices, on_device(): lax.all_to_all(spread_rows(value_blocks, devices), 'ctx', split_axis=1, c...  18.5 us
    all_to_all x1, waiting for transfers between devices, on_device(): lax.all_to_all(spread_rows(value_terms[:, 2 * BLOCK:], devices), 'ctx', s...  16.3 us
    all_to_all x1, waiting for transfers between devices, on_device(): lax.all_to_all(choose_pieces(arrived[1], pairing, devices), 'ctx', split_...  13.2 us
    all_to_all x1, waiting for transfers between devices, on_device(): lax.all_to_all(choose_pieces(arrived[0], pairing, devices), 'ctx', split_...  12.6 us
  transfers between devices with their start and end apart: 11, of which 8 were waited for; matrix products, arithmetic and copies ran while one was open for 9% of the time, Pallas kernels for 0%

commit v1 on v0

v1 whole, which is shorter than its diff:
```python
import functools
import math

import jax
import jax.numpy as jnp
from jax import lax
from jax.experimental import pallas as pl
from jax.experimental.pallas import tpu as pltpu
from jax.sharding import PartitionSpec as P

HD = 128
ROWS = 16
EPSILON = 1e-05
MESH = pl.DeviceIdType.MESH
F32 = jnp.float32
BF16 = jnp.bfloat16


def mm(a, b, da, db):
    return lax.dot_general(a, b, (((da,), (db,)), ((), ())), preferred_element_type=F32)


def body(
    sizes,
    q_in,
    k_in,
    v_in,
    c_in,
    gain,
    pairing,
    inverse,
    mixed_out,
    gq_out,
    gk_out,
    gv_out,
    qh,
    kh,
    vh,
    ch,
    pk,
    pv,
    k1,
    v1,
    k2,
    v2,
    k3,
    v3,
    bkp,
    bvp,
    bkn,
    bvn,
    nk,
    nv,
    k4,
    v4,
    k5,
    v5,
    k6,
    v6,
    win,
    probs,
    dsc,
    acc,
    gin,
    att,
    dat,
    delta,
    stats,
    own_k,
    own_v,
    load_sem,
    send_sem,
    recv_sem,
):
    Z, X, G = sizes
    N = Z * X
    B = Z * ROWS
    factor = 1.0 / math.sqrt(HD)
    features = float(G * X * HD)
    ctx = lax.axis_index("ctx")
    hd = lax.axis_index("head")
    z = ctx // X
    x = lax.rem(ctx, X)
    mine = x * Z + z
    after = lax.rem(ctx + 1, N)
    before = lax.rem(ctx + N - 1, N)

    def peer(k):
        return lax.rem(z + k // X, Z) * X + lax.rem(x + k, X)

    def slot_of(j):
        return lax.rem(j, X) * Z + j // X

    def lanes(h):
        return pl.ds(pl.multiple_of(h * HD, HD), HD)

    def head_rows(h):
        return pl.ds(pl.multiple_of(h * Z, Z), Z)

    def block(ref, h):
        return ref[head_rows(h)].reshape(B, HD)

    def remote(src, dst, n, j, g):
        return pltpu.make_async_remote_copy(
            src_ref=src,
            dst_ref=dst,
            send_sem=send_sem.at[n],
            recv_sem=recv_sem.at[n],
            device_id=(j, g),
            device_id_type=MESH,
        )

    def loop(lo, hi, f):
        def step(k, carry):
            f(k)
            return carry

        lax.fori_loop(lo, hi, step, 0)

    def await_bytes(ref, sem):
        pltpu.make_async_copy(ref, ref, sem).wait()

    barrier = pltpu.get_barrier_semaphore()
    loop(
        1,
        N,
        lambda k: pl.semaphore_signal(
            barrier, inc=1, device_id=(peer(k), hd), device_id_type=MESH
        ),
    )
    loop(
        1,
        G,
        lambda k: pl.semaphore_signal(
            barrier, inc=1, device_id=(ctx, lax.rem(hd + k, G)), device_id_type=MESH
        ),
    )

    loads = []
    for n, (src, dst) in enumerate(((k_in, kh), (v_in, vh), (q_in, qh), (c_in, ch))):
        for h in range(X):
            copy = pltpu.make_async_copy(
                src.at[:, :, pl.ds(h * HD, HD)],
                dst.at[pl.ds(h * Z, Z)],
                load_sem.at[n * X + h],
            )
            copy.start()
            loads.append(copy)
    for copy in loads:
        copy.wait()
    k1[ctx] = kh[mine]
    v1[ctx] = vh[mine]
    pl.semaphore_wait(barrier, N - 1 + G - 1)

    loop(1, N, lambda k: remote(kh.at[slot_of(peer(k))], k1.at[ctx], 0, peer(k), hd).start())
    to_next_k = remote(kh, pk, 8, after, hd)
    to_next_k.start()
    loop(1, N, lambda k: remote(vh.at[slot_of(peer(k))], v1.at[ctx], 1, peer(k), hd).start())
    to_next_v = remote(vh, pv, 9, after, hd)
    to_next_v.start()

    def own_scores(h):
        s = mm(block(kh, h), block(qh, h), 1, 1) * factor
        key_at = lax.broadcasted_iota(jnp.int32, (B, B), 0)
        query_at = lax.broadcasted_iota(jnp.int32, (B, B), 1)
        win[h, pl.ds(B, B)] = jnp.where(key_at <= query_at, s, -jnp.inf)
        grad_in = block(ch, h).astype(F32) * gain[:, lanes(h)]
        gin[h] = grad_in.T

    loop(0, X, own_scores)

    def choose(dst, src, table):
        def f(j):
            dst[j] = src[table[j]]

        loop(0, N, f)

    def forward(src, dst, n):
        dst[mine] = src[ctx]
        loop(1, N, lambda k: remote(src.at[peer(k)], dst.at[mine], n, peer(k), hd).start())

    def await_pieces(dst, n):
        await_bytes(dst.at[pl.ds(0, N - 1)], recv_sem.at[n])

    await_pieces(k1, 0)
    choose(k2, k1, pairing)
    forward(k2, k3, 2)
    await_pieces(v1, 1)
    choose(v2, v1, pairing)
    forward(v2, v3, 3)

    to_next_k.wait_recv()

    def prior_scores(h):
        s = mm(block(pk, h), block(qh, h), 1, 1) * factor
        win[h, pl.ds(0, B)] = jnp.where(ctx > 0, s, -jnp.inf)

    loop(0, X, prior_scores)
    to_next_v.wait_recv()
    await_pieces(k3, 2)

    def softmax(h):
        win[h, pl.ds(2 * B, B)] = mm(block(k3, h), block(qh, h), 1, 1) * factor
        s = win[h]
        highest = jnp.max(s, axis=0, keepdims=True)
        logsum = highest + jnp.log(jnp.sum(jnp.exp(s - highest), axis=0, keepdims=True))
        w = jnp.exp(s - logsum)
        win[h] = w
        p = w.astype(BF16)
        probs[h] = p
        acc[h] = mm(block(pv, h), p[0:B], 0, 0) + mm(block(vh, h), p[B : 2 * B], 0, 0)

    loop(0, X, softmax)
    await_pieces(v3, 3)

    stats[hd] = jnp.zeros((8, B), F32)

    def attend(h):
        o = acc[h] + mm(block(v3, h), probs[h, pl.ds(2 * B, B)], 0, 0)
        a = o.astype(BF16).astype(F32)
        att[h] = a
        stats[hd, 0:1] += jnp.sum(a * a, axis=0, keepdims=True)
        stats[hd, 1:2] += jnp.sum(gin[h] * a, axis=0, keepdims=True)

    loop(0, X, attend)
    loop(
        1,
        G,
        lambda k: remote(stats.at[hd], stats.at[hd], 10, ctx, lax.rem(hd + k, G)).start(),
    )
    await_bytes(stats.at[pl.ds(0, G - 1)], recv_sem.at[10])
    total = jnp.sum(stats[...], axis=0)
    rms = lax.rsqrt(total[0:1] / features + EPSILON)
    slope = rms * rms * rms * (total[1:2] / features)

    def value_terms(k):
        h = lax.rem(x + k, X)
        a = att[h]
        d = (rms * gin[h] - a * slope).astype(BF16)
        dat[h] = d
        delta[h] = jnp.sum(d.astype(F32) * a, axis=0, keepdims=True)
        term = mm(probs[h, pl.ds(2 * B, B)], d, 1, 1).astype(BF16)
        bvp[head_rows(h)] = term.reshape(Z, ROWS, HD)

        def send(n):
            zj = lax.rem(z + n, Z)
            j = zj * X + h

            @pl.when(j != ctx)
            def _():
                remote(bvp.at[h * Z + zj], v4.at[ctx], 5, j, hd).start()

        loop(0, Z, send)

    loop(0, X, value_terms)
    v4[ctx] = bvp[mine]

    def score_grad(h, g, values):
        dp = mm(values, dat[h], 1, 0)
        d = (win[h, pl.ds(g * B, B)] * (dp - delta[h])).astype(BF16)
        dsc[h, pl.ds(g * B, B)] = d
        return d

    def key_terms(k):
        h = lax.rem(x + k, X)
        d = score_grad(h, 2, block(v3, h))
        term = (mm(d, block(qh, h), 1, 0) * factor).astype(BF16)
        bkp[head_rows(h)] = term.reshape(Z, ROWS, HD)

        def send(n):
            zj = lax.rem(z + n, Z)
            j = zj * X + h

            @pl.when(j != ctx)
            def _():
                remote(bkp.at[h * Z + zj], k4.at[ctx], 4, j, hd).start()

        loop(0, Z, send)

    loop(0, X, key_terms)
    k4[ctx] = bkp[mine]

    def prior_terms(h):
        d = score_grad(h, 0, block(pv, h))
        term = (mm(d, block(qh, h), 1, 0) * factor).astype(BF16)
        bkn[head_rows(h)] = term.reshape(Z, ROWS, HD)
        term = mm(probs[h, pl.ds(0, B)], dat[h], 1, 1).astype(BF16)
        bvn[head_rows(h)] = term.reshape(Z, ROWS, HD)

    loop(0, X, prior_terms)
    to_prior_v = remote(bvn, nv, 11, before, hd)
    to_prior_v.start()
    to_prior_k = remote(bkn, nk, 12, before, hd)
    to_prior_k.start()

    def own_terms(h):
        d = score_grad(h, 1, block(vh, h))
        own_k[h] = (mm(d, block(qh, h), 1, 0) * factor).astype(BF16).astype(F32)
        own_v[h] = mm(probs[h, pl.ds(B, B)], dat[h], 1, 1).astype(BF16).astype(F32)
        gq = (
            mm(dsc[h, pl.ds(0, B)], block(pk, h), 0, 0)
            + mm(dsc[h, pl.ds(B, B)], block(kh, h), 0, 0)
            + mm(dsc[h, pl.ds(2 * B, B)], block(k3, h), 0, 0)
        )
        gq_out[:, lanes(h)] = (gq * factor).astype(BF16)
        mixed_out[:, lanes(h)] = ((att[h] * rms).T * gain[:, lanes(h)]).astype(BF16)

    loop(0, X, own_terms)

    await_pieces(v4, 5)
    choose(v5, v4, inverse)
    forward(v5, v6, 7)
    await_pieces(k4, 4)
    choose(k5, k4, inverse)
    forward(k5, k6, 6)

    to_prior_v.wait_recv()
    to_prior_k.wait_recv()

    def add_next(h):
        own_v[h] += block(nv, h).astype(F32)
        own_k[h] += block(nk, h).astype(F32)

    loop(0, X, add_next)
    await_pieces(v6, 7)

    def give_v(h):
        gv_out[:, lanes(h)] = (own_v[h] + block(v6, h).astype(F32)).astype(BF16)

    loop(0, X, give_v)
    await_pieces(k6, 6)

    def give_k(h):
        gk_out[:, lanes(h)] = (own_k[h] + block(k6, h).astype(F32)).astype(BF16)

    loop(0, X, give_k)

    for n in range(8):
        await_bytes(k1.at[pl.ds(0, N - 1)], send_sem.at[n])
    await_bytes(stats.at[pl.ds(0, G - 1)], send_sem.at[10])
    for copy in (to_next_k, to_next_v, to_prior_v, to_prior_k):
        copy.wait_send()


def on_device(sizes, queries, key_rows, value_rows, cotangent, norm_gain, pairing):
    Z, X, G = sizes
    N, B, W = Z * X, Z * ROWS, X * HD
    tiles = (Z, ROWS, W)
    places = jnp.arange(N, dtype=jnp.int32)
    inverse = jnp.sum(
        jnp.where(pairing[None, :] == places[:, None], places[None, :], 0), axis=1
    ).astype(jnp.int32)
    vmem = pl.BlockSpec(memory_space=pltpu.VMEM)
    smem = pl.BlockSpec(memory_space=pltpu.SMEM)
    hbm = pl.BlockSpec(memory_space=pl.ANY)
    pieces = pltpu.VMEM((N, ROWS, HD), BF16)
    square = pltpu.VMEM((X, HD, B), F32)
    out = jax.ShapeDtypeStruct((B, W), BF16)
    return pl.pallas_call(
        functools.partial(body, sizes),
        out_shape=(out,) * 4,
        in_specs=[hbm] * 4 + [vmem, smem, smem],
        out_specs=(vmem,) * 4,
        scratch_shapes=[pieces] * 24
        + [
            pltpu.VMEM((X, 3 * B, B), F32),
            pltpu.VMEM((X, 3 * B, B), BF16),
            pltpu.VMEM((X, 3 * B, B), BF16),
            square,
            square,
            square,
            pltpu.VMEM((X, HD, B), BF16),
            pltpu.VMEM((X, 1, B), F32),
            pltpu.VMEM((G, 8, B), F32),
            pltpu.VMEM((X, B, HD), F32),
            pltpu.VMEM((X, B, HD), F32),
            pltpu.SemaphoreType.DMA((4 * X,)),
            pltpu.SemaphoreType.DMA((13,)),
            pltpu.SemaphoreType.DMA((13,)),
        ],
        compiler_params=pltpu.CompilerParams(
            collective_id=0, has_side_effects=True, vmem_limit_bytes=48 << 20
        ),
    )(
        queries.reshape(tiles),
        key_rows.reshape(tiles),
        value_rows.reshape(tiles),
        cotangent.reshape(tiles),
        norm_gain.reshape(1, W),
        pairing,
        inverse,
    )


def solution(mesh):
    heads_here = 4
    sizes = (mesh.shape["ctx"] // heads_here, heads_here, mesh.shape["head"])
    spec = P("ctx", "head")
    return jax.shard_map(
        functools.partial(on_device, sizes),
        mesh=mesh,
        in_specs=(spec, spec, spec, spec, P("head"), P()),
        out_specs=(spec,) * 4,
        check_vma=False,
    )
```

time: 272 us -> 153 us (0.56)
  Pallas kernels: 0 us -> 144 us
  waiting for transfers between devices: 110 us -> 0 us
  starting transfers between devices: 67 us -> 0 us
  blocking collectives: 38.8 us -> 0 us
  local copies, waits for them, and re-layouts: 28.9 us -> 7.25 us
  matrix products: 12.8 us -> 0 us
  other arithmetic: 12 us -> 0.11 us
    pallas_call x0 -> x1, Pallas kernels: none -> 144 us  [on_device(): pl.pallas_call(functools.partial(body, sizes), out_shape=(out,) * 4, in_s...]
    all_to_all x7 -> x0, waiting for transfers between devices: 108 us -> none  [the longest x1 19.8 us: on_device(): lax.all_to_all(spread_rows(key_blocks, devices), 'ctx', split_axis=1, con...]
    all_to_all x7 -> x0, starting transfers between devices: 55.1 us -> none  [the longest x1 18.6 us: on_device(): lax.all_to_all(spread_rows(key_blocks, devices), 'ctx', split_axis=1, con...]
    all_to_all x1 -> x0, blocking collectives: 26.4 us -> none  [on_device(): lax.all_to_all(choose_pieces(returned[0], inverse, devices), 'ctx', split...]
    dot_general x6 -> x0, matrix products: 12.8 us -> none  [the longest x1 2.99 us: on_device(): jnp.einsum('bhij,bjhd->bihd', weights_low, values_window, preferred_eleme...]
    psum x1 -> x0, blocking collectives: 12.4 us -> none  [on_device(): lax.psum((jnp.sum(attn_flat * attn_flat, axis=1), jnp.sum(grad_in * attn_...]
    ppermute x4 -> x0, starting transfers between devices: 12 us -> none  [from_behind(): lax.ppermute(value, axis, [(source, source + steps) for source in range(f...]
    concatenate x8 -> x0, local copies, waits for them, and re-layouts: 5.4 us -> none  [the longest x2 3.56 us: on_device(): jnp.concatenate([prior_values, value_blocks, partner_values], axis=1)]
  transfers between devices with their start and end apart: 11 -> 0, of which waited for: 8 -> 0; matrix products, arithmetic and copies ran while one was open for 9% -> 0% of each run, Pallas kernels for 0% -> 0%
where the time goes in v1:
time: 153 us; the launch traced here: 152 us
  Pallas kernels  144 us (94%)
  local copies, waits for them, and re-layouts  7.25 us (5%)
    pallas_call x1, Pallas kernels, on_device(): pl.pallas_call(functools.partial(body, sizes), out_shape=(out,) * 4, in_s...  144 us
    unnamed x16, local copies, waits for them, and re-layouts  7.25 us

profile of v1, /device:TPU:6, one launch (start us, length us, event | category | flops | bytes accessed | tf_op | source)
XLA Modules:
  0.0 152.1 jit_solution(12540191753054454182)
XLA Ops:
  0.6 0.0 copy-start.5
  0.6 0.0 copy-start.4
  0.7 0.6 copy-done.5
  1.3 0.1 select_reduce_fusion.inverse
  1.4 0.0 copy-done.4
  1.4 0.0 copy-start
  1.4 0.9 copy-done
  2.4 0.0 copy-start.1
  2.4 0.9 copy-done.1
  3.3 0.0 copy-start.2
  3.3 0.9 copy-done.2
  4.3 0.0 copy-start.3
  4.3 0.9 copy-done.3
  5.2 144.0 %shard_map.93 = (bf16[256,512]{1,0:T(8,128)(2,1)S(1)}, bf16[256,512]{1,0:T(8,128)(2,1)S(1)}, bf16[256,512]{1,0:T(8,128)(2,1)S(1)}, bf16[256,512]{1,0:T(8,128)(2,1)S(1)}) custom-call(bf16[16,16,512]{2,1,0:T(8,128)(2,1)S(1)} %bitcast.5, bf16[16,16,512]{2,1,0:T(8,128)(2,1)S(1)} %bitcast.6, bf16[16,16,512]{2,1,0:T(8,128)(2,1)S(1)} %bitcast.7, ...), custom_call_target="tpu_custom_call" | custom-call | tf_op jit(solution)/shard_map/pallas_call | solution.py:359
  149.2 0.7 copy.14
  149.9 0.7 copy.15
  150.7 0.7 copy.16
  151.4 0.7 copy.17
Async XLA Ops:
  0.6 0.7 copy-start.5
  0.6 0.8 copy-start.4
  1.4 1.0 copy-start
  2.4 0.9 copy-start.1
  3.3 0.9 copy-start.2
  4.3 0.9 copy-start.3

commit v2 on v1

--- a/solution.py
+++ b/solution.py
@@ -26,9 +26,8 @@
     k_in,
     v_in,
     c_in,
-    gain,
-    pairing,
-    inverse,
+    gain_in,
+    pairing_in,
     mixed_out,
     gq_out,
     gk_out,
@@ -68,6 +67,15 @@
     stats,
     own_k,
     own_v,
+    rk,
+    rv,
+    rkb,
+    rvb,
+    gain,
+    pair_row,
+    inverse_row,
+    pairing,
+    inverse,
     load_sem,
     send_sem,
     recv_sem,
@@ -100,12 +108,12 @@
     def block(ref, h):
         return ref[head_rows(h)].reshape(B, HD)
 
-    def remote(src, dst, n, j, g):
+    def remote(src, dst, n, j, g, m=None):
         return pltpu.make_async_remote_copy(
             src_ref=src,
             dst_ref=dst,
             send_sem=send_sem.at[n],
-            recv_sem=recv_sem.at[n],
+            recv_sem=recv_sem.at[n if m is None else m],
             device_id=(j, g),
             device_id_type=MESH,
         )
@@ -136,6 +144,13 @@
         ),
     )
 
+    small = (
+        pltpu.make_async_copy(gain_in, gain, load_sem.at[4 * X]),
+        pltpu.make_async_copy(pairing_in, pair_row, load_sem.at[4 * X + 1]),
+        pltpu.make_async_copy(pairing_in, pairing, load_sem.at[4 * X + 2]),
+    )
+    for copy in small:
+        copy.start()
     loads = []
     for n, (src, dst) in enumerate(((k_in, kh), (v_in, vh), (q_in, qh), (c_in, ch))):
         for h in range(X):
@@ -146,18 +161,56 @@
             )
             copy.start()
             loads.append(copy)
+    for copy in small:
+        copy.wait()
+    down = lax.broadcasted_iota(jnp.int32, (N, N), 0)
+    across = lax.broadcasted_iota(jnp.int32, (N, N), 1)
+    partners = jnp.broadcast_to(pair_row[...], (N, N))
+    partner_of = jnp.sum(jnp.where(down == across, partners, 0), axis=1, keepdims=True)
+    inverse_row[...] = jnp.max(jnp.where(partner_of == across, down, 0), axis=0, keepdims=True)
+    turn = pltpu.make_async_copy(inverse_row, inverse, load_sem.at[4 * X + 3])
+    turn.start()
     for copy in loads:
         copy.wait()
+    turn.wait()
     k1[ctx] = kh[mine]
     v1[ctx] = vh[mine]
     pl.semaphore_wait(barrier, N - 1 + G - 1)
 
+    def pass_on(src, relay, dst, n, edge, step, target):
+        @pl.when(x != edge)
+        def _():
+            remote(src, dst, n, target, hd).start()
+
+        @pl.when(x == edge)
+        def _():
+            for h in range(1, X):
+                via = edge + h * step
+                part = pl.ds(via * Z, Z)
+                remote(src.at[part], relay, n, z * X + via, hd, n + 2).start()
+            part = pl.ds(edge * Z, Z)
+            remote(src.at[part], dst.at[part], n, target, hd).start()
+
+    def relay_on(relay, dst, n, edge, target):
+        @pl.when(x != edge)
+        def _():
+            await_bytes(relay, recv_sem.at[n + 2])
+            remote(relay, dst.at[head_rows(x)], n + 2, target, hd, n).start()
+
+    def end_pass(src, relay, n, edge):
+        await_bytes(src, send_sem.at[n])
+
+        @pl.when(x != edge)
+        def _():
+            await_bytes(relay, send_sem.at[n + 2])
+
+    over = lax.rem(z + 1, Z) * X
+    under = lax.rem(z + Z - 1, Z) * X + X - 1
+
     loop(1, N, lambda k: remote(kh.at[slot_of(peer(k))], k1.at[ctx], 0, peer(k), hd).start())
-    to_next_k = remote(kh, pk, 8, after, hd)
-    to_next_k.start()
+    pass_on(kh, rk, pk, 8, X - 1, -1, after)
     loop(1, N, lambda k: remote(vh.at[slot_of(peer(k))], v1.at[ctx], 1, peer(k), hd).start())
-    to_next_v = remote(vh, pv, 9, after, hd)
-    to_next_v.start()
+    pass_on(vh, rv, pv, 9, X - 1, -1, after)
 
     def own_scores(h):
         s = mm(block(kh, h), block(qh, h), 1, 1) * factor
@@ -171,7 +224,7 @@
 
     def choose(dst, src, table):
         def f(j):
-            dst[j] = src[table[j]]
+            dst[j] = src[table[0, j]]
 
         loop(0, N, f)
 
@@ -185,18 +238,20 @@
     await_pieces(k1, 0)
     choose(k2, k1, pairing)
     forward(k2, k3, 2)
+    relay_on(rk, pk, 8, X - 1, over)
     await_pieces(v1, 1)
     choose(v2, v1, pairing)
     forward(v2, v3, 3)
-
-    to_next_k.wait_recv()
+    relay_on(rv, pv, 9, X - 1, over)
+
+    await_bytes(pk, recv_sem.at[8])
 
     def prior_scores(h):
         s = mm(block(pk, h), block(qh, h), 1, 1) * factor
         win[h, pl.ds(0, B)] = jnp.where(ctx > 0, s, -jnp.inf)
 
     loop(0, X, prior_scores)
-    to_next_v.wait_recv()
+    await_bytes(pv, recv_sem.at[9])
     await_pieces(k3, 2)
 
     def softmax(h):
@@ -226,9 +281,9 @@
     loop(
         1,
         G,
-        lambda k: remote(stats.at[hd], stats.at[hd], 10, ctx, lax.rem(hd + k, G)).start(),
-    )
-    await_bytes(stats.at[pl.ds(0, G - 1)], recv_sem.at[10])
+        lambda k: remote(stats.at[hd], stats.at[hd], 12, ctx, lax.rem(hd + k, G)).start(),
+    )
+    await_bytes(stats.at[pl.ds(0, G - 1)], recv_sem.at[12])
     total = jnp.sum(stats[...], axis=0)
     rms = lax.rsqrt(total[0:1] / features + EPSILON)
     slope = rms * rms * rms * (total[1:2] / features)
@@ -288,10 +343,8 @@
         bvn[head_rows(h)] = term.reshape(Z, ROWS, HD)
 
     loop(0, X, prior_terms)
-    to_prior_v = remote(bvn, nv, 11, before, hd)
-    to_prior_v.start()
-    to_prior_k = remote(bkn, nk, 12, before, hd)
-    to_prior_k.start()
+    pass_on(bvn, rvb, nv, 13, 0, 1, before)
+    pass_on(bkn, rkb, nk, 14, 0, 1, before)
 
     def own_terms(h):
         d = score_grad(h, 1, block(vh, h))
@@ -310,12 +363,14 @@
     await_pieces(v4, 5)
     choose(v5, v4, inverse)
     forward(v5, v6, 7)
+    relay_on(rvb, nv, 13, 0, under)
+    relay_on(rkb, nk, 14, 0, under)
     await_pieces(k4, 4)
     choose(k5, k4, inverse)
     forward(k5, k6, 6)
 
-    to_prior_v.wait_recv()
-    to_prior_k.wait_recv()
+    await_bytes(nv, recv_sem.at[13])
+    await_bytes(nk, recv_sem.at[14])
 
     def add_next(h):
         own_v[h] += block(nv, h).astype(F32)
@@ -337,29 +392,36 @@
 
     for n in range(8):
         await_bytes(k1.at[pl.ds(0, N - 1)], send_sem.at[n])
-    await_bytes(stats.at[pl.ds(0, G - 1)], send_sem.at[10])
-    for copy in (to_next_k, to_next_v, to_prior_v, to_prior_k):
-        copy.wait_send()
+    await_bytes(stats.at[pl.ds(0, G - 1)], send_sem.at[12])
+    end_pass(kh, rk, 8, X - 1)
+    end_pass(vh, rv, 9, X - 1)
+    end_pass(bvn, rvb, 13, 0)
+    end_pass(bkn, rkb, 14, 0)
+
+
+def write_out(*refs):
+    sem = refs[8]
+    copies = [pltpu.make_async_copy(refs[n], refs[4 + n], sem.at[n]) for n in range(4)]
+    for copy in copies:
+        copy.start()
+    for copy in copies:
+        copy.wait()
 
 
 def on_device(sizes, queries, key_rows, value_rows, cotangent, norm_gain, pairing):
     Z, X, G = sizes
     N, B, W = Z * X, Z * ROWS, X * HD
     tiles = (Z, ROWS, W)
-    places = jnp.arange(N, dtype=jnp.int32)
-    inverse = jnp.sum(
-        jnp.where(pairing[None, :] == places[:, None], places[None, :], 0), axis=1
-    ).astype(jnp.int32)
     vmem = pl.BlockSpec(memory_space=pltpu.VMEM)
-    smem = pl.BlockSpec(memory_space=pltpu.SMEM)
-    hbm = pl.BlockSpec(memory_space=pl.ANY)
+    hbm = pl.BlockSpec(memory_space=pltpu.HBM)
+    part = pltpu.VMEM((Z, ROWS, HD), BF16)
     pieces = pltpu.VMEM((N, ROWS, HD), BF16)
     square = pltpu.VMEM((X, HD, B), F32)
     out = jax.ShapeDtypeStruct((B, W), BF16)
-    return pl.pallas_call(
+    held = pl.pallas_call(
         functools.partial(body, sizes),
         out_shape=(out,) * 4,
-        in_specs=[hbm] * 4 + [vmem, smem, smem],
+        in_specs=[hbm] * 6,
         out_specs=(vmem,) * 4,
         scratch_shapes=[pieces] * 24
         + [
@@ -374,12 +436,21 @@
             pltpu.VMEM((G, 8, B), F32),
             pltpu.VMEM((X, B, HD), F32),
             pltpu.VMEM((X, B, HD), F32),
-            pltpu.SemaphoreType.DMA((4 * X,)),
-            pltpu.SemaphoreType.DMA((13,)),
-            pltpu.SemaphoreType.DMA((13,)),
+            part,
+            part,
+            part,
+            part,
+            pltpu.VMEM((1, W), F32),
+            pltpu.VMEM((1, N), jnp.int32),
+            pltpu.VMEM((1, N), jnp.int32),
+            pltpu.SMEM((1, N), jnp.int32),
+            pltpu.SMEM((1, N), jnp.int32),
+            pltpu.SemaphoreType.DMA((4 * X + 4,)),
+            pltpu.SemaphoreType.DMA((17,)),
+            pltpu.SemaphoreType.DMA((17,)),
         ],
         compiler_params=pltpu.CompilerParams(
-            collective_id=0, has_side_effects=True, vmem_limit_bytes=48 << 20
+            collective_id=0, has_side_effects=True, vmem_limit_bytes=56 << 20
         ),
     )(
         queries.reshape(tiles),
@@ -387,9 +458,15 @@
         value_rows.reshape(tiles),
         cotangent.reshape(tiles),
         norm_gain.reshape(1, W),
-        pairing,
-        inverse,
-    )
+        pairing.reshape(1, N),
+    )
+    return pl.pallas_call(
+        write_out,
+        out_shape=(out,) * 4,
+        in_specs=[vmem] * 4,
+        out_specs=(hbm,) * 4,
+        scratch_shapes=[pltpu.SemaphoreType.DMA((4,))],
+    )(*held)
 
 
 def solution(mesh):

time: 153 us -> 135 us (0.88); the launches traced: 152 us -> 132 us
  Pallas kernels: 144 us -> 132 us
  local copies, waits for them, and re-layouts: 7.25 us -> 0 us
    pallas_call x1, Pallas kernels: 144 us -> 130 us  [on_device(): pl.pallas_call(functools.partial(body, sizes), out_shape=(out,) * 4, in_s...]
    unnamed x16 -> x0, local copies, waits for them, and re-layouts: 7.25 us -> none
    pallas_call x0 -> x1, Pallas kernels: none -> 2.18 us  [on_device(): pl.pallas_call(write_out, out_shape=(out,) * 4, in_specs=[vmem] * 4, out_...]
where the time goes in v2:
time: 135 us; the launch traced here: 132 us
  Pallas kernels  132 us (98%)
    pallas_call x1, Pallas kernels, on_device(): pl.pallas_call(functools.partial(body, sizes), out_shape=(out,) * 4, in_s...  130 us

profile of v2, /device:TPU:6, one launch (start us, length us, event | category | flops | bytes accessed | tf_op | source)
XLA Modules:
  0.0 132.4 jit_solution(5057892770488632099)
XLA Ops:
  0.6 129.6 %shard_map.93 = (bf16[256,512]{1,0:T(8,128)(2,1)}, bf16[256,512]{1,0:T(8,128)(2,1)}, bf16[256,512]{1,0:T(8,128)(2,1)}, bf16[256,512]{1,0:T(8,128)(2,1)}) custom-call(bf16[16,16,512]{2,1,0:T(8,128)(2,1)} %bitcast.6, bf16[16,16,512]{2,1,0:T(8,128)(2,1)} %bitcast.7, bf16[16,16,512]{2,1,0:T(8,128)(2,1)} %bitcast.8, bf16[16,16,512]{2,1,0:T(8,128)(2,1)} %bitcast.9, ...), custom_call_target="tpu_custom_call" | custom-call | tf_op jit(solution)/shard_map/pallas_call | solution.py:421
  130.2 2.2 %shard_map.94 = (bf16[256,512]{1,0:T(8,128)(2,1)}, bf16[256,512]{1,0:T(8,128)(2,1)}, bf16[256,512]{1,0:T(8,128)(2,1)}, bf16[256,512]{1,0:T(8,128)(2,1)}) custom-call(bf16[256,512]{1,0:T(8,128)(2,1)} %get-tuple-element.8.refs_0_, bf16[256,512]{1,0:T(8,128)(2,1)} %get-tuple-element.9.refs_1_, bf16[256,512]{1,0:T(8,128)(2,1)} %get-tuple-element.10.refs_2_, ...), custom_call_target="tpu_custom_call" | custom-call | tf_op jit(solution)/shard_map/pallas_call | solution.py:463

commit v3 on v2

v3 whole, which is shorter than its diff:
```python
import functools
import math
import types

import jax
import jax.numpy as jnp
from jax import lax
from jax.experimental import pallas as pl
from jax.experimental.pallas import tpu as pltpu
from jax.sharding import PartitionSpec as P

HD = 128
ROWS = 16
EPSILON = 1e-05
MESH = pl.DeviceIdType.MESH
F32 = jnp.float32
BF16 = jnp.bfloat16

K_ONE, V_ONE, Q_ONE, D_ONE, K_TWO, V_TWO, Q_TWO, D_TWO = range(8)
PASS_K, PASS_V, RELAY_K, RELAY_V, BACK_V, BACK_K, RELAY_BV, RELAY_BK, STATS, E_ONE, E_TWO, HEAD = range(8, 20)


def mm(a, b, da, db):
    return lax.dot_general(a, b, (((da,), (db,)), ((), ())), preferred_element_type=F32)


def scratch(sizes):
    Z, X, G = sizes
    N, B, W = Z * X, Z * ROWS, X * HD
    pieces = pltpu.VMEM((N, ROWS, HD), BF16)
    part = pltpu.VMEM((Z, ROWS, HD), BF16)
    turned = pltpu.VMEM((X, HD, B), F32)
    upright = pltpu.VMEM((X, B, HD), F32)
    return dict(
        qh=pieces, kh=pieces, vh=pieces, ch=pieces,
        k1=pieces, v1=pieces, q1=pieces, d1=pieces,
        k2=pieces, v2=pieces, q2=pieces, d2=pieces,
        k3=pieces, v3=pieces, q3=pieces, d3=pieces,
        d0=pieces, pk=pieces, pv=pieces, bk=pieces, bv=pieces, nk=pieces, nv=pieces,
        rk=part, rv=part, rbk=part, rbv=part,
        win=pltpu.VMEM((X, 3 * B, B), F32),
        probs=pltpu.VMEM((X, 3 * B, B), BF16),
        dsc=pltpu.VMEM((X, 3 * B, B), BF16),
        win_in=pltpu.VMEM((X, B, B), F32),
        probs_in=pltpu.VMEM((X, B, B), BF16),
        acc=turned, gin=turned, att=turned,
        dat=pltpu.VMEM((X, HD, B), BF16),
        delta=pltpu.VMEM((X, 1, B), F32),
        lse=pltpu.VMEM((X, 1, B), F32),
        stats=pltpu.VMEM((G, 8, B), F32),
        e0=pltpu.VMEM((2 * X, 2, B // 2), F32),
        e1=pltpu.VMEM((N, 2, B // 2), F32),
        e2=pltpu.VMEM((N, 2, B // 2), F32),
        e3=pltpu.VMEM((2 * X, 2, B // 2), F32),
        own_k=upright, own_v=upright,
        gain=pltpu.VMEM((1, W), F32),
        pair_row=pltpu.VMEM((1, N), jnp.int32),
        inverse_row=pltpu.VMEM((1, N), jnp.int32),
        pairing=pltpu.SMEM((1, N), jnp.int32),
        inverse=pltpu.SMEM((1, N), jnp.int32),
        load_sem=pltpu.SemaphoreType.DMA((4 * X + 4,)),
        send_sem=pltpu.SemaphoreType.DMA((HEAD,)),
        recv_sem=pltpu.SemaphoreType.DMA((HEAD + X,)),
    )


def body(sizes, q_in, k_in, v_in, c_in, gain_in, pairing_in, mixed_out, gq_out, gk_out, gv_out, *refs):
    s = types.SimpleNamespace(**dict(zip(scratch(sizes), refs)))
    Z, X, G = sizes
    N = Z * X
    B = Z * ROWS
    half = B // 2
    factor = 1.0 / math.sqrt(HD)
    features = float(G * X * HD)
    ctx = lax.axis_index("ctx")
    hd = lax.axis_index("head")
    z = ctx // X
    x = lax.rem(ctx, X)

    def wrap(i, n):
        return jnp.where(i >= n, i - n, i)

    after = wrap(ctx + 1, N)
    before = wrap(ctx + N - 1, N)
    over = wrap(z + 1, Z) * X
    under = wrap(z + Z - 1, Z) * X + X - 1
    columns = [wrap(x + n, X) for n in range(X)]

    def via(h, zj):
        return zj * X + 2 * lax.rem(h, 2) + lax.rem(zj + h // 2, 2)

    my_head = 2 * lax.rem(x + z, 2) + x // 2
    mine = my_head * Z + z

    def lanes(h):
        return pl.ds(pl.multiple_of(h * HD, HD), HD)

    def head_rows(h):
        return pl.ds(pl.multiple_of(h * Z, Z), Z)

    def block(ref, h):
        return ref[head_rows(h)].reshape(B, HD)

    def remote(src, dst, n, j, g, m=None):
        return pltpu.make_async_remote_copy(
            src_ref=src,
            dst_ref=dst,
            send_sem=s.send_sem.at[n],
            recv_sem=s.recv_sem.at[n if m is None else m],
            device_id=(j, g),
            device_id_type=MESH,
        )

    def loop(lo, hi, f):
        def step(k, carry):
            f(k)
            return carry

        lax.fori_loop(lo, hi, step, 0)

    def each_peer(f):
        for n in range(1, X):
            f(z * X + columns[n])

        def along_z(k):
            zj = wrap(z + k, Z)
            for n in range(X):
                f(zj * X + columns[n])

        loop(1, Z, along_z)

    def each_head_peer(f):
        loop(1, G, lambda k: f(wrap(hd + k, G)))

    def await_bytes(ref, sem):
        pltpu.make_async_copy(ref, ref, sem).wait()

    barrier = pltpu.get_barrier_semaphore()
    each_peer(lambda j: pl.semaphore_signal(barrier, inc=1, device_id=(j, hd), device_id_type=MESH))
    each_head_peer(lambda g: pl.semaphore_signal(barrier, inc=1, device_id=(ctx, g), device_id_type=MESH))

    small = (
        pltpu.make_async_copy(pairing_in, s.pair_row, s.load_sem.at[4 * X + 1]),
        pltpu.make_async_copy(pairing_in, s.pairing, s.load_sem.at[4 * X + 2]),
        pltpu.make_async_copy(gain_in, s.gain, s.load_sem.at[4 * X]),
    )
    loads = []
    for n, (src, dst) in enumerate(((k_in, s.kh), (v_in, s.vh), (q_in, s.qh), (c_in, s.ch))):
        for h in range(X):
            loads.append(
                pltpu.make_async_copy(
                    src.at[:, :, pl.ds(h * HD, HD)], dst.at[pl.ds(h * Z, Z)], s.load_sem.at[n * X + h]
                )
            )
    for copy in loads[:X] + list(small) + loads[X:]:
        copy.start()
    for copy in small:
        copy.wait()
    down = lax.broadcasted_iota(jnp.int32, (N, N), 0)
    across = lax.broadcasted_iota(jnp.int32, (N, N), 1)
    partners = jnp.broadcast_to(s.pair_row[...], (N, N))
    partner_of = jnp.sum(jnp.where(down == across, partners, 0), axis=1, keepdims=True)
    s.inverse_row[...] = jnp.max(jnp.where(partner_of == across, down, 0), axis=0, keepdims=True)
    turn = pltpu.make_async_copy(s.inverse_row, s.inverse, s.load_sem.at[4 * X + 3])
    turn.start()
    for copy in loads:
        copy.wait()
    turn.wait()
    s.k1[ctx] = s.kh[mine]
    s.v1[ctx] = s.vh[mine]
    s.q1[ctx] = s.qh[mine]
    pl.semaphore_wait(barrier, N - 1 + G - 1)

    def pass_on(src, relay, dst, n, edge, step, target):
        @pl.when(x != edge)
        def _():
            remote(src, dst, n, target, hd).start()

        @pl.when(x == edge)
        def _():
            for h in range(1, X):
                by = edge + h * step
                part = pl.ds(by * Z, Z)
                remote(src.at[part], relay, n, z * X + by, hd, n + 2).start()
            part = pl.ds(edge * Z, Z)
            remote(src.at[part], dst.at[part], n, target, hd).start()

    def relay_on(relay, dst, n, edge, target):
        @pl.when(x != edge)
        def _():
            await_bytes(relay, s.recv_sem.at[n + 2])
            remote(relay, dst.at[head_rows(x)], n + 2, target, hd, n).start()

    def end_pass(src, relay, n, edge):
        await_bytes(src, s.send_sem.at[n])

        @pl.when(x != edge)
        def _():
            await_bytes(relay, s.send_sem.at[n + 2])

    def spread(src, dst, n):
        def of_head(h):
            def to(k):
                zj = wrap(z + k, Z)
                j = via(h, zj)

                @pl.when(j != ctx)
                def _():
                    remote(src.at[h * Z + zj], dst.at[ctx], n, j, hd).start()

            loop(0, Z, to)

        loop(0, X, of_head)

    def choose(dst, src, table):
        def f(j):
            dst[j] = src[table[0, j]]

        loop(0, N, f)

    def forward(src, dst, n):
        dst[mine] = src[ctx]
        each_peer(lambda j: remote(src.at[j], dst.at[mine], n, j, hd).start())

    def await_pieces(dst, n):
        await_bytes(dst.at[pl.ds(0, N - 1)], s.recv_sem.at[n])

    spread(s.kh, s.k1, K_ONE)
    pass_on(s.kh, s.rk, s.pk, PASS_K, X - 1, -1, after)
    spread(s.vh, s.v1, V_ONE)
    pass_on(s.vh, s.rv, s.pv, PASS_V, X - 1, -1, after)
    spread(s.qh, s.q1, Q_ONE)

    def own_scores(h):
        score = mm(block(s.kh, h), block(s.qh, h), 1, 1) * factor
        key_at = lax.broadcasted_iota(jnp.int32, (B, B), 0)
        query_at = lax.broadcasted_iota(jnp.int32, (B, B), 1)
        s.win[h, pl.ds(B, B)] = jnp.where(key_at <= query_at, score, -jnp.inf)
        s.gin[h] = (block(s.ch, h).astype(F32) * s.gain[:, lanes(h)]).T

    loop(0, X, own_scores)

    await_pieces(s.k1, K_ONE)
    choose(s.k2, s.k1, s.pairing)
    forward(s.k2, s.k3, K_TWO)
    relay_on(s.rk, s.pk, PASS_K, X - 1, over)
    await_pieces(s.v1, V_ONE)
    choose(s.v2, s.v1, s.pairing)
    forward(s.v2, s.v3, V_TWO)
    relay_on(s.rv, s.pv, PASS_V, X - 1, over)
    await_pieces(s.q1, Q_ONE)
    choose(s.q2, s.q1, s.inverse)
    forward(s.q2, s.q3, Q_TWO)

    await_bytes(s.pk, s.recv_sem.at[PASS_K])

    def prior_scores(h):
        score = mm(block(s.pk, h), block(s.qh, h), 1, 1) * factor
        s.win[h, pl.ds(0, B)] = jnp.where(ctx > 0, score, -jnp.inf)

    loop(0, X, prior_scores)
    await_bytes(s.pv, s.recv_sem.at[PASS_V])
    await_pieces(s.k3, K_TWO)

    def softmax(h):
        s.win[h, pl.ds(2 * B, B)] = mm(block(s.k3, h), block(s.qh, h), 1, 1) * factor
        score = s.win[h]
        highest = jnp.max(score, axis=0, keepdims=True)
        logsum = highest + jnp.log(jnp.sum(jnp.exp(score - highest), axis=0, keepdims=True))
        s.lse[h] = logsum
        w = jnp.exp(score - logsum)
        s.win[h] = w
        p = w.astype(BF16)
        s.probs[h] = p
        s.acc[h] = mm(block(s.pv, h), p[0:B], 0, 0) + mm(block(s.vh, h), p[B : 2 * B], 0, 0)

    loop(0, X, softmax)
    s.stats[hd] = jnp.zeros((8, B), F32)
    await_pieces(s.v3, V_TWO)

    def attend(h):
        o = s.acc[h] + mm(block(s.v3, h), s.probs[h, pl.ds(2 * B, B)], 0, 0)
        a = o.astype(BF16).astype(F32)
        s.att[h] = a
        s.stats[hd, 0:1] += jnp.sum(a * a, axis=0, keepdims=True)
        s.stats[hd, 1:2] += jnp.sum(s.gin[h] * a, axis=0, keepdims=True)

    loop(0, X, attend)
    each_head_peer(lambda g: remote(s.stats.at[hd], s.stats.at[hd], STATS, ctx, g).start())
    await_bytes(s.stats.at[pl.ds(0, G - 1)], s.recv_sem.at[STATS])
    total = jnp.sum(s.stats[...], axis=0)
    rms = lax.rsqrt(total[0:1] / features + EPSILON)
    slope = rms * rms * rms * (total[1:2] / features)

    def attn_grad(h):
        a = s.att[h]
        d = rms * s.gin[h] - a * slope
        low = d.astype(BF16)
        s.dat[h] = low
        s.d0[head_rows(h)] = d.T.astype(BF16).reshape(Z, ROWS, HD)
        delta = jnp.sum(low.astype(F32) * a, axis=0, keepdims=True)
        s.delta[h] = delta
        logsum = s.lse[h]
        for t in range(2):
            cut = slice(t * half, (t + 1) * half)
            s.e0[2 * h + t, 0:1] = logsum[:, cut]
            s.e0[2 * h + t, 1:2] = delta[:, cut]

    loop(0, X, attn_grad)

    rows = 2 * X
    gap = (N - 1) // (rows - 1)
    row = ctx // gap
    carries = ctx == row * gap
    for r in range(rows):

        @pl.when(ctx != r * gap)
        def _():
            remote(s.e0.at[r], s.e1.at[ctx], E_ONE, r * gap, hd).start()

        @pl.when(ctx == r * gap)
        def _():
            pltpu.make_async_copy(s.e0.at[r], s.e1.at[ctx], s.recv_sem.at[E_ONE]).start()

    s.d1[ctx] = s.d0[mine]
    spread(s.d0, s.d1, D_ONE)

    def score_grad(h, g, values):
        dp = mm(values, s.dat[h], 1, 0)
        d = (s.win[h, pl.ds(g * B, B)] * (dp - s.delta[h])).astype(BF16)
        s.dsc[h, pl.ds(g * B, B)] = d
        return d

    def prior_terms(h):
        d = score_grad(h, 0, block(s.pv, h))
        term = (mm(d, block(s.qh, h), 1, 0) * factor).astype(BF16)
        s.bk[head_rows(h)] = term.reshape(Z, ROWS, HD)
        term = mm(s.probs[h, pl.ds(0, B)], s.dat[h], 1, 1).astype(BF16)
        s.bv[head_rows(h)] = term.reshape(Z, ROWS, HD)

    loop(0, X, prior_terms)
    pass_on(s.bv, s.rbv, s.nv, BACK_V, 0, 1, before)
    pass_on(s.bk, s.rbk, s.nk, BACK_K, 0, 1, before)

    @pl.when(carries)
    def _():
        await_bytes(s.e1, s.recv_sem.at[E_ONE])
        choose(s.e2, s.e1, s.inverse)
        each_peer(lambda j: remote(s.e2.at[j], s.e3.at[row], E_TWO, j, hd).start())
        pltpu.make_async_copy(s.e2.at[ctx], s.e3.at[row], s.recv_sem.at[E_TWO]).start()

    def own_terms(h):
        d = score_grad(h, 1, block(s.vh, h))
        s.own_k[h] = mm(d, block(s.qh, h), 1, 0) * factor
        s.own_v[h] = mm(s.probs[h, pl.ds(B, B)], s.dat[h], 1, 1)

    loop(0, X, own_terms)

    await_pieces(s.d1, D_ONE)
    choose(s.d2, s.d1, s.inverse)
    each_peer(lambda j: remote(s.d2.at[j], s.d3.at[mine], D_TWO, j, hd, HEAD + my_head).start())
    pltpu.make_async_copy(s.d2.at[ctx], s.d3.at[mine], s.recv_sem.at[HEAD + my_head]).start()
    relay_on(s.rbv, s.nv, BACK_V, 0, under)
    relay_on(s.rbk, s.nk, BACK_K, 0, under)

    def query_terms(h):
        d = score_grad(h, 2, block(s.v3, h))
        gq = (
            mm(s.dsc[h, pl.ds(0, B)], block(s.pk, h), 0, 0)
            + mm(s.dsc[h, pl.ds(B, B)], block(s.kh, h), 0, 0)
            + mm(d, block(s.k3, h), 0, 0)
        )
        gq_out[:, lanes(h)] = (gq * factor).astype(BF16)
        mixed_out[:, lanes(h)] = ((s.att[h] * rms).T * s.gain[:, lanes(h)]).astype(BF16)

    loop(0, X, query_terms)

    await_pieces(s.q3, Q_TWO)
    await_bytes(s.e3, s.recv_sem.at[E_TWO])

    def incoming(h, n):
        return jnp.concatenate([s.e3[2 * h, n : n + 1], s.e3[2 * h + 1, n : n + 1]], axis=1)

    def incoming_probs(h):
        w = jnp.exp(mm(block(s.kh, h), block(s.q3, h), 1, 1) * factor - incoming(h, 0))
        s.win_in[h] = w
        s.probs_in[h] = w.astype(BF16)

    loop(0, X, incoming_probs)
    await_bytes(s.nv, s.recv_sem.at[BACK_V])
    await_bytes(s.nk, s.recv_sem.at[BACK_K])

    def add_next(h):
        s.own_v[h] += block(s.nv, h).astype(F32)
        s.own_k[h] += block(s.nk, h).astype(F32)

    loop(0, X, add_next)

    def partner_terms(h):
        await_bytes(s.d3.at[head_rows(h)], s.recv_sem.at[HEAD + h])
        d = block(s.d3, h)
        gv_out[:, lanes(h)] = (s.own_v[h] + mm(s.probs_in[h], d, 1, 0)).astype(BF16)
        dp = mm(block(s.vh, h), d, 1, 1)
        ds = (s.win_in[h] * (dp - incoming(h, 1))).astype(BF16)
        gk_out[:, lanes(h)] = (s.own_k[h] + mm(ds, block(s.q3, h), 1, 0) * factor).astype(BF16)

    loop(0, X, partner_terms)

    for n in (K_ONE, V_ONE, Q_ONE, D_ONE, K_TWO, V_TWO, Q_TWO, D_TWO):
        await_bytes(s.k1.at[pl.ds(0, N - 1)], s.send_sem.at[n])
    await_bytes(s.stats.at[pl.ds(0, G - 1)], s.send_sem.at[STATS])
    end_pass(s.kh, s.rk, PASS_K, X - 1)
    end_pass(s.vh, s.rv, PASS_V, X - 1)
    end_pass(s.bv, s.rbv, BACK_V, 0)
    end_pass(s.bk, s.rbk, BACK_K, 0)

    @pl.when(carries)
    def _():
        await_bytes(s.e0.at[pl.ds(0, rows - 1)], s.send_sem.at[E_ONE])
        await_bytes(s.e2.at[pl.ds(0, N - 1)], s.send_sem.at[E_TWO])

    @pl.when(jnp.logical_not(carries))
    def _():
        await_bytes(s.e0, s.send_sem.at[E_ONE])


def write_out(*refs):
    sem = refs[8]
    copies = [pltpu.make_async_copy(refs[n], refs[4 + n], sem.at[n]) for n in range(4)]
    for copy in copies:
        copy.start()
    for copy in copies:
        copy.wait()


def on_device(sizes, queries, key_rows, value_rows, cotangent, norm_gain, pairing):
    Z, X, G = sizes
    N, B, W = Z * X, Z * ROWS, X * HD
    tiles = (Z, ROWS, W)
    hbm = pl.BlockSpec(memory_space=pltpu.HBM)
    out = jax.ShapeDtypeStruct((B, W), BF16)
    held = pl.pallas_call(
        functools.partial(body, sizes),
        out_shape=(pltpu.VMEM((B, W), BF16),) * 4,
        in_specs=[hbm] * 6,
        out_specs=(pl.BlockSpec(memory_space=pltpu.VMEM),) * 4,
        scratch_shapes=list(scratch(sizes).values()),
        compiler_params=pltpu.CompilerParams(
            collective_id=0, has_side_effects=True, vmem_limit_bytes=56 << 20
        ),
    )(
        queries.reshape(tiles),
        key_rows.reshape(tiles),
        value_rows.reshape(tiles),
        cotangent.reshape(tiles),
        norm_gain.reshape(1, W),
        pairing.reshape(1, N),
    )
    return pl.pallas_call(
        write_out,
        out_shape=(out,) * 4,
        in_specs=[pl.BlockSpec(memory_space=pltpu.VMEM)] * 4,
        out_specs=(hbm,) * 4,
        scratch_shapes=[pltpu.SemaphoreType.DMA((4,))],
        compiler_params=pltpu.CompilerParams(vmem_limit_bytes=4 << 20),
    )(*held)


def solution(mesh):
    heads_here = 4
    sizes = (mesh.shape["ctx"] // heads_here, heads_here, mesh.shape["head"])
    spec = P("ctx", "head")
    return jax.shard_map(
        functools.partial(on_device, sizes),
        mesh=mesh,
        in_specs=(spec, spec, spec, spec, P("head"), P()),
        out_specs=(spec,) * 4,
        check_vma=False,
    )
```

time: 135 us -> 124 us (0.919); the launches traced: 132 us -> 123 us
  Pallas kernels: 132 us -> 122 us
    pallas_call x2, Pallas kernels: 132 us -> 122 us  [the longest x1 121 us: on_device(): pl.pallas_call(functools.partial(body, sizes), out_shape=(pltpu.VMEM((B,...]
where the time goes in v3:
time: 124 us; the launch traced here: 123 us
  Pallas kernels  122 us (98%)
    pallas_call x1, Pallas kernels, on_device(): pl.pallas_call(functools.partial(body, sizes), out_shape=(pltpu.VMEM((B,...  121 us

profile of v3, /device:TPU:6, one launch (start us, length us, event | category | flops | bytes accessed | tf_op | source)
XLA Modules:
  0.0 122.8 jit_solution(12161756340178157597)
XLA Ops:
  0.6 121.1 %shard_map.93 = (bf16[256,512]{1,0:T(8,128)(2,1)S(1)}, bf16[256,512]{1,0:T(8,128)(2,1)S(1)}, bf16[256,512]{1,0:T(8,128)(2,1)S(1)}, bf16[256,512]{1,0:T(8,128)(2,1)S(1)}) custom-call(bf16[16,16,512]{2,1,0:T(8,128)(2,1)} %bitcast.6, bf16[16,16,512]{2,1,0:T(8,128)(2,1)} %bitcast.7, bf16[16,16,512]{2,1,0:T(8,128)(2,1)} %bitcast.8, bf16[16,16,512]{2,1,0:T(8,128)(2,1)} %bitcast.9, ...), custom_call_target="tpu_custom_call" | custom-call | tf_op jit(solution)/shard_map/pallas_call | solution.py:442
  121.8 1.0 shard_map.94

commit v4 on v3

--- a/solution.py
+++ b/solution.py
@@ -229,7 +229,6 @@
     pass_on(s.kh, s.rk, s.pk, PASS_K, X - 1, -1, after)
     spread(s.vh, s.v1, V_ONE)
     pass_on(s.vh, s.rv, s.pv, PASS_V, X - 1, -1, after)
-    spread(s.qh, s.q1, Q_ONE)
 
     def own_scores(h):
         score = mm(block(s.kh, h), block(s.qh, h), 1, 1) * factor
@@ -248,9 +247,7 @@
     choose(s.v2, s.v1, s.pairing)
     forward(s.v2, s.v3, V_TWO)
     relay_on(s.rv, s.pv, PASS_V, X - 1, over)
-    await_pieces(s.q1, Q_ONE)
-    choose(s.q2, s.q1, s.inverse)
-    forward(s.q2, s.q3, Q_TWO)
+    spread(s.qh, s.q1, Q_ONE)
 
     await_bytes(s.pk, s.recv_sem.at[PASS_K])
 
@@ -324,6 +321,10 @@
 
     s.d1[ctx] = s.d0[mine]
     spread(s.d0, s.d1, D_ONE)
+
+    await_pieces(s.q1, Q_ONE)
+    choose(s.q2, s.q1, s.inverse)
+    forward(s.q2, s.q3, Q_TWO)
 
     def score_grad(h, g, values):
         dp = mm(values, s.dat[h], 1, 0)

time: 124 us -> 121 us (0.976)
  Pallas kernels: 122 us -> 120 us
    pallas_call x1, Pallas kernels: 121 us -> 119 us  [on_device(): pl.pallas_call(functools.partial(body, sizes), out_shape=(pltpu.VMEM((B,...]
where the time goes in v4:
time: 121 us
  Pallas kernels  120 us (99%)
    pallas_call x1, Pallas kernels, on_device(): pl.pallas_call(functools.partial(body, sizes), out_shape=(pltpu.VMEM((B,...  119 us

profile of v4, /device:TPU:6, one launch (start us, length us, event | category | flops | bytes accessed | tf_op | source)
XLA Modules:
  0.0 120.8 jit_solution(9524764986084011296)
XLA Ops:
  0.6 119.1 %shard_map.93 = (bf16[256,512]{1,0:T(8,128)(2,1)S(1)}, bf16[256,512]{1,0:T(8,128)(2,1)S(1)}, bf16[256,512]{1,0:T(8,128)(2,1)S(1)}, bf16[256,512]{1,0:T(8,128)(2,1)S(1)}) custom-call(bf16[16,16,512]{2,1,0:T(8,128)(2,1)} %bitcast.6, bf16[16,16,512]{2,1,0:T(8,128)(2,1)} %bitcast.7, bf16[16,16,512]{2,1,0:T(8,128)(2,1)} %bitcast.8, bf16[16,16,512]{2,1,0:T(8,128)(2,1)} %bitcast.9, ...), custom_call_target="tpu_custom_call" | custom-call | tf_op jit(solution)/shard_map/pallas_call | solution.py:443
  119.8 1.0 shard_map.94

commit v5 on v4

--- a/solution.py
+++ b/solution.py
@@ -47,7 +47,7 @@
         dat=pltpu.VMEM((X, HD, B), BF16),
         delta=pltpu.VMEM((X, 1, B), F32),
         lse=pltpu.VMEM((X, 1, B), F32),
-        stats=pltpu.VMEM((G, 8, B), F32),
+        stats=pltpu.VMEM((G, 2, B), F32),
         e0=pltpu.VMEM((2 * X, 2, B // 2), F32),
         e1=pltpu.VMEM((N, 2, B // 2), F32),
         e2=pltpu.VMEM((N, 2, B // 2), F32),
@@ -60,7 +60,7 @@
         inverse=pltpu.SMEM((1, N), jnp.int32),
         load_sem=pltpu.SemaphoreType.DMA((4 * X + 4,)),
         send_sem=pltpu.SemaphoreType.DMA((HEAD,)),
-        recv_sem=pltpu.SemaphoreType.DMA((HEAD + X,)),
+        recv_sem=pltpu.SemaphoreType.DMA((HEAD + 2 * X,)),
     )
 
 
@@ -198,19 +198,19 @@
         def _():
             await_bytes(relay, s.send_sem.at[n + 2])
 
+    def spread_head(src, dst, n, h):
+        def to(k):
+            zj = wrap(z + k, Z)
+            j = via(h, zj)
+
+            @pl.when(j != ctx)
+            def _():
+                remote(src.at[h * Z + zj], dst.at[ctx], n, j, hd).start()
+
+        loop(0, Z, to)
+
     def spread(src, dst, n):
-        def of_head(h):
-            def to(k):
-                zj = wrap(z + k, Z)
-                j = via(h, zj)
-
-                @pl.when(j != ctx)
-                def _():
-                    remote(src.at[h * Z + zj], dst.at[ctx], n, j, hd).start()
-
-            loop(0, Z, to)
-
-        loop(0, X, of_head)
+        loop(0, X, lambda h: spread_head(src, dst, n, h))
 
     def choose(dst, src, table):
         def f(j):
@@ -245,7 +245,8 @@
     relay_on(s.rk, s.pk, PASS_K, X - 1, over)
     await_pieces(s.v1, V_ONE)
     choose(s.v2, s.v1, s.pairing)
-    forward(s.v2, s.v3, V_TWO)
+    each_peer(lambda j: remote(s.v2.at[j], s.v3.at[mine], V_TWO, j, hd, HEAD + X + my_head).start())
+    pltpu.make_async_copy(s.v2.at[ctx], s.v3.at[mine], s.recv_sem.at[HEAD + X + my_head]).start()
     relay_on(s.rv, s.pv, PASS_V, X - 1, over)
     spread(s.qh, s.q1, Q_ONE)
 
@@ -272,10 +273,10 @@
         s.acc[h] = mm(block(s.pv, h), p[0:B], 0, 0) + mm(block(s.vh, h), p[B : 2 * B], 0, 0)
 
     loop(0, X, softmax)
-    s.stats[hd] = jnp.zeros((8, B), F32)
-    await_pieces(s.v3, V_TWO)
+    s.stats[hd] = jnp.zeros((2, B), F32)
 
     def attend(h):
+        await_bytes(s.v3.at[head_rows(h)], s.recv_sem.at[HEAD + X + h])
         o = s.acc[h] + mm(block(s.v3, h), s.probs[h, pl.ds(2 * B, B)], 0, 0)
         a = o.astype(BF16).astype(F32)
         s.att[h] = a
@@ -295,6 +296,7 @@
         low = d.astype(BF16)
         s.dat[h] = low
         s.d0[head_rows(h)] = d.T.astype(BF16).reshape(Z, ROWS, HD)
+        spread_head(s.d0, s.d1, D_ONE, h)
         delta = jnp.sum(low.astype(F32) * a, axis=0, keepdims=True)
         s.delta[h] = delta
         logsum = s.lse[h]
@@ -320,7 +322,6 @@
             pltpu.make_async_copy(s.e0.at[r], s.e1.at[ctx], s.recv_sem.at[E_ONE]).start()
 
     s.d1[ctx] = s.d0[mine]
-    spread(s.d0, s.d1, D_ONE)
 
     await_pieces(s.q1, Q_ONE)
     choose(s.q2, s.q1, s.inverse)

time: 121 us -> 120 us (level)
  no operation moved by 1% of the time
where the time goes in v5:
time: 120 us
  Pallas kernels  119 us (99%)
    pallas_call x1, Pallas kernels, on_device(): pl.pallas_call(functools.partial(body, sizes), out_shape=(pltpu.VMEM((B,...  118 us

profile of v5, /device:TPU:6, one launch (start us, length us, event | category | flops | bytes accessed | tf_op | source)
XLA Modules:
  0.0 119.7 jit_solution(12435567455704115601)
XLA Ops:
  0.6 118.1 %shard_map.93 = (bf16[256,512]{1,0:T(8,128)(2,1)S(1)}, bf16[256,512]{1,0:T(8,128)(2,1)S(1)}, bf16[256,512]{1,0:T(8,128)(2,1)S(1)}, bf16[256,512]{1,0:T(8,128)(2,1)S(1)}) custom-call(bf16[16,16,512]{2,1,0:T(8,128)(2,1)} %bitcast.6, bf16[16,16,512]{2,1,0:T(8,128)(2,1)} %bitcast.7, bf16[16,16,512]{2,1,0:T(8,128)(2,1)} %bitcast.8, bf16[16,16,512]{2,1,0:T(8,128)(2,1)} %bitcast.9, ...), custom_call_target="tpu_custom_call" | custom-call | tf_op jit(solution)/shard_map/pallas_call | solution.py:444
  118.7 1.0 shard_map.94

commit v6 on v5

--- a/solution.py
+++ b/solution.py
@@ -154,8 +154,76 @@
             )
     for copy in loads[:X] + list(small) + loads[X:]:
         copy.start()
-    for copy in small:
+    for copy in loads[:X]:
         copy.wait()
+    s.k1[ctx] = s.kh[mine]
+    pl.semaphore_wait(barrier, N - 1 + G - 1)
+
+    def pass_on(src, relay, dst, n, edge, step, target):
+        @pl.when(x != edge)
+        def _():
+            remote(src, dst, n, target, hd).start()
+
+        @pl.when(x == edge)
+        def _():
+            for h in range(1, X):
+                by = edge + h * step
+                part = pl.ds(by * Z, Z)
+                remote(src.at[part], relay, n, z * X + by, hd, n + 2).start()
+            part = pl.ds(edge * Z, Z)
+            remote(src.at[part], dst.at[part], n, target, hd).start()
+
+    def relay_on(relay, dst, n, edge, target):
+        @pl.when(x != edge)
+        def _():
+            await_bytes(relay, s.recv_sem.at[n + 2])
+            remote(relay, dst.at[head_rows(x)], n + 2, target, hd, n).start()
+
+    def end_pass(src, relay, n, edge):
+        await_bytes(src, s.send_sem.at[n])
+
+        @pl.when(x != edge)
+        def _():
+            await_bytes(relay, s.send_sem.at[n + 2])
+
+    def spread_head(src, dst, n, h):
+        def to(k):
+            zj = wrap(z + k, Z)
+            j = via(h, zj)
+
+            @pl.when(j != ctx)
+            def _():
+                remote(src.at[h * Z + zj], dst.at[ctx], n, j, hd).start()
+
+        loop(0, Z, to)
+
+    def spread(src, dst, n):
+        loop(0, X, lambda h: spread_head(src, dst, n, h))
+
+    def choose(dst, src, table):
+        def f(j):
+            dst[j] = src[table[0, j]]
+
+        loop(0, N, f)
+
+    def forward(src, dst, n):
+        dst[mine] = src[ctx]
+        each_peer(lambda j: remote(src.at[j], dst.at[mine], n, j, hd).start())
+
+    def await_pieces(dst, n):
+        await_bytes(dst.at[pl.ds(0, N - 1)], s.recv_sem.at[n])
+
+    spread(s.kh, s.k1, K_ONE)
+    pass_on(s.kh, s.rk, s.pk, PASS_K, X - 1, -1, after)
+    for copy in loads[X : 2 * X]:
+        copy.wait()
+    s.v1[ctx] = s.vh[mine]
+    spread(s.vh, s.v1, V_ONE)
+    pass_on(s.vh, s.rv, s.pv, PASS_V, X - 1, -1, after)
+
+    for copy in list(small) + loads[2 * X :]:
+        copy.wait()
+    s.q1[ctx] = s.qh[mine]
     down = lax.broadcasted_iota(jnp.int32, (N, N), 0)
     across = lax.broadcasted_iota(jnp.int32, (N, N), 1)
     partners = jnp.broadcast_to(s.pair_row[...], (N, N))
@@ -163,72 +231,6 @@
     s.inverse_row[...] = jnp.max(jnp.where(partner_of == across, down, 0), axis=0, keepdims=True)
     turn = pltpu.make_async_copy(s.inverse_row, s.inverse, s.load_sem.at[4 * X + 3])
     turn.start()
-    for copy in loads:
-        copy.wait()
-    turn.wait()
-    s.k1[ctx] = s.kh[mine]
-    s.v1[ctx] = s.vh[mine]
-    s.q1[ctx] = s.qh[mine]
-    pl.semaphore_wait(barrier, N - 1 + G - 1)
-
-    def pass_on(src, relay, dst, n, edge, step, target):
-        @pl.when(x != edge)
-        def _():
-            remote(src, dst, n, target, hd).start()
-
-        @pl.when(x == edge)
-        def _():
-            for h in range(1, X):
-                by = edge + h * step
-                part = pl.ds(by * Z, Z)
-                remote(src.at[part], relay, n, z * X + by, hd, n + 2).start()
-            part = pl.ds(edge * Z, Z)
-            remote(src.at[part], dst.at[part], n, target, hd).start()
-
-    def relay_on(relay, dst, n, edge, target):
-        @pl.when(x != edge)
-        def _():
-            await_bytes(relay, s.recv_sem.at[n + 2])
-            remote(relay, dst.at[head_rows(x)], n + 2, target, hd, n).start()
-
-    def end_pass(src, relay, n, edge):
-        await_bytes(src, s.send_sem.at[n])
-
-        @pl.when(x != edge)
-        def _():
-            await_bytes(relay, s.send_sem.at[n + 2])
-
-    def spread_head(src, dst, n, h):
-        def to(k):
-            zj = wrap(z + k, Z)
-            j = via(h, zj)
-
-            @pl.when(j != ctx)
-            def _():
-                remote(src.at[h * Z + zj], dst.at[ctx], n, j, hd).start()
-
-        loop(0, Z, to)
-
-    def spread(src, dst, n):
-        loop(0, X, lambda h: spread_head(src, dst, n, h))
-
-    def choose(dst, src, table):
-        def f(j):
-            dst[j] = src[table[0, j]]
-
-        loop(0, N, f)
-
-    def forward(src, dst, n):
-        dst[mine] = src[ctx]
-        each_peer(lambda j: remote(src.at[j], dst.at[mine], n, j, hd).start())
-
-    def await_pieces(dst, n):
-        await_bytes(dst.at[pl.ds(0, N - 1)], s.recv_sem.at[n])
-
-    spread(s.kh, s.k1, K_ONE)
-    pass_on(s.kh, s.rk, s.pk, PASS_K, X - 1, -1, after)
-    spread(s.vh, s.v1, V_ONE)
-    pass_on(s.vh, s.rv, s.pv, PASS_V, X - 1, -1, after)
 
     def own_scores(h):
         score = mm(block(s.kh, h), block(s.qh, h), 1, 1) * factor
@@ -238,6 +240,7 @@
         s.gin[h] = (block(s.ch, h).astype(F32) * s.gain[:, lanes(h)]).T
 
     loop(0, X, own_scores)
+    turn.wait()
 
     await_pieces(s.k1, K_ONE)
     choose(s.k2, s.k1, s.pairing)

time: 120 us -> 120 us (level)
  no operation moved by 1% of the time
where the time goes in v6:
time: 120 us
  Pallas kernels  119 us (99%)
    pallas_call x1, Pallas kernels, on_device(): pl.pallas_call(functools.partial(body, sizes), out_shape=(pltpu.VMEM((B,...  118 us

profile of v6, /device:TPU:6, one launch (start us, length us, event | category | flops | bytes accessed | tf_op | source)
XLA Modules:
  0.0 119.7 jit_solution(10462592955562970567)
XLA Ops:
  0.6 118.1 %shard_map.93 = (bf16[256,512]{1,0:T(8,128)(2,1)S(1)}, bf16[256,512]{1,0:T(8,128)(2,1)S(1)}, bf16[256,512]{1,0:T(8,128)(2,1)S(1)}, bf16[256,512]{1,0:T(8,128)(2,1)S(1)}) custom-call(bf16[16,16,512]{2,1,0:T(8,128)(2,1)} %bitcast.6, bf16[16,16,512]{2,1,0:T(8,128)(2,1)} %bitcast.7, bf16[16,16,512]{2,1,0:T(8,128)(2,1)} %bitcast.8, bf16[16,16,512]{2,1,0:T(8,128)(2,1)} %bitcast.9, ...), custom_call_target="tpu_custom_call" | custom-call | tf_op jit(solution)/shard_map/pallas_call | solution.py:447
  118.7 1.0 shard_map.94
